TPU v7x, 256 devices: a whole 4x4x8 slice. The times are simulated.
256 devices in a mesh: seq: 16 (over z_lo, x), head: 16 (over z_hi, y, core).
Axes of the slice: x: 4, y: 4, z: 8 (z_hi: 2, z_lo: 4; z = z_hi * 4 + z_lo), core: 2. Of those that a mesh axis runs over, the one named last changes fastest.
Arguments:
- query_in: bfloat16 [8192, 3072], P(('seq', 'head')), may hold values from -160 to 160
- key_in: bfloat16 [8192, 3072], P(('seq', 'head')), may hold values from -6 to 6
- value_in: bfloat16 [8192, 3072], P(('seq', 'head')), may hold values from -6 to 6
- block_mask: int32 [9, 4, 4], replicated, may hold values from 0 to 1, as said below
- out_weight: bfloat16 [3072, 3072], P('head'), may hold values from -0.109375 to 0.109375
- out_bias: bfloat16 [3072], replicated, may hold values from -3 to 3
Outputs:
- layer_out: bfloat16 [8192, 3072], P(('seq', 'head'))
Inputs may be any that keep to these rules, and one draw needn't show every extreme that they name: `block_mask`: entry 0 has ones on its diagonal tiles; every entry holds at least one 1; entries 2l - 1 and 2l keep about a 2**l-th of their tiles.
All inputs are finite; a program needn't handle non-finite values.
Results may differ from a plain program's by a relative error of at most 0.0027.
Values may be sent and summed in bfloat16 or wider, within the bound.
A program may use at most 128 MiB of HBM per device.

v0:
```python
import math

import jax
import jax.numpy as jnp
from jax import lax
from jax.sharding import PartitionSpec as P

HD = 64


def shifted(value, axis, steps):
    count = lax.axis_size(axis)
    first, last = (max(0, -steps), min(count, count - steps))
    return lax.ppermute(value, axis, [(source, source + steps) for source in range(first, last)])


def expand_mask(tile_mask, tile_rows):
    return jnp.repeat(jnp.repeat(tile_mask, tile_rows, axis=0), tile_rows, axis=1) > 0


def fetch_pair(keys_local, values_local, offset):
    return shifted((keys_local, values_local), "seq", -offset)


def shards(query_in, key_in, value_in, block_mask, out_weight, out_bias):
    local_query, local_keys, local_values = (
        lax.all_to_all(query_in, "head", split_axis=1, concat_axis=0, tiled=True),
        lax.all_to_all(key_in, "head", split_axis=1, concat_axis=0, tiled=True),
        lax.all_to_all(value_in, "head", split_axis=1, concat_axis=0, tiled=True),
    )
    tok_rows = local_query.shape[0]
    head_count = local_query.shape[1] // HD
    seq_count = lax.axis_size("seq")
    seq_index = lax.axis_index("seq")
    tile_rows = tok_rows // block_mask.shape[1]
    score_scale = 1.0 / math.sqrt(HD)
    level_total = min(4, 3 + seq_count // 16)
    block_plan = [(0, 0)]
    for level_no in range(1, level_total + 1):
        span = 2 ** (level_no - 1)
        block_plan.append((-span, 2 * level_no - 1))
        block_plan.append((span, 2 * level_no))
    present = []
    for offset, mask_index in block_plan:
        if offset == 0:
            present.append((local_keys, local_values, offset, mask_index))
        else:
            keys_here, values_here = fetch_pair(local_keys, local_values, offset)
            present.append((keys_here, values_here, offset, mask_index))
    queries = local_query.reshape(tok_rows, head_count, HD)
    prepared = []
    top = jnp.full((head_count, tok_rows), -jnp.inf, jnp.float32)
    for keys_here, values_here, offset, mask_index in present:
        inside = (seq_index + offset >= 0) & (seq_index + offset < seq_count)
        keep_map = expand_mask(block_mask[mask_index], tile_rows) & inside
        scores = (
            jnp.einsum(
                "qhd,khd->hqk",
                queries,
                keys_here.reshape(tok_rows, head_count, HD),
                preferred_element_type=jnp.float32,
            )
            * score_scale
        )
        scores = jnp.where(keep_map[None], scores, -jnp.inf)
        top = jnp.maximum(top, jnp.max(scores, axis=2))
        prepared.append((scores, values_here.reshape(tok_rows, head_count, HD), keep_map))
    total = jnp.zeros((head_count, tok_rows), jnp.float32)
    summed = jnp.zeros((tok_rows, head_count, HD), jnp.float32)
    for scores, values_here, keep_map in prepared:
        weights = jnp.where(keep_map[None], jnp.exp(scores - top[:, :, None]), jnp.float32(0.0))
        total = total + jnp.sum(weights, axis=2)
        summed = summed + jnp.einsum(
            "hqk,khd->qhd",
            weights.astype(jnp.bfloat16),
            values_here,
            preferred_element_type=jnp.float32,
        )
    attended = (
        (summed / jnp.transpose(total)[:, :, None])
        .astype(jnp.bfloat16)
        .reshape(tok_rows, head_count * HD)
    )
    projected = lax.psum_scatter(
        jnp.dot(attended, out_weight, preferred_element_type=jnp.float32),
        "head",
        scatter_dimension=0,
        tiled=True,
    )
    return (projected + out_bias.astype(jnp.float32)[None, :]).astype(jnp.bfloat16)


def solution(mesh):
    return jax.shard_map(
        shards,
        mesh=mesh,
        in_specs=(
            P(("seq", "head"), None),
            P(("seq", "head"), None),
            P(("seq", "head"), None),
            P(),
            P("head", None),
            P(),
        ),
        out_specs=P(("seq", "head"), None),
        check_vma=False,
    )
```

profile of v0, /device:TPU:1, one launch (start us, length us, event | category | flops | bytes accessed | tf_op | source)
XLA Modules:
  0.0 334.3 jit_solution(9533026003636246498)
XLA Ops:
  6.5 1.4 all_to_all.40
  8.7 12.6 %all-to-all-start = ((bf16[32,16,192]{2,0,1:T(8,128)(2,1)}), bf16[32,16,192]{2,0,1:T(8,128)(2,1)S(1)}, u32[]{:S(2)}, u32[]{:S(2)}) async-start(bf16[32,16,192]{2,0,1:T(8,128)(2,1)} %copy.29), calls=%async_computation | async-start | bytes 524288 | tf_op jit(solution)/shard_map/all_to_all | solution.py:27
  22.6 1.2 all_to_all.43
  25.7 6.7 %all-to-all-done = bf16[32,16,192]{2,0,1:T(8,128)(2,1)S(1)} async-done(((bf16[32,16,192]{2,0,1:T(8,128)(2,1)}), bf16[32,16,192]{2,0,1:T(8,128)(2,1)S(1)}, u32[]{:S(2)}, u32[]{:S(2)}) %all-to-all-start) | async-done | bytes 196640 | tf_op jit(solution)/shard_map/all_to_all | solution.py:27
  32.4 4.4 %all-to-all-start.1 = ((bf16[32,16,192]{2,0,1:T(8,128)(2,1)}), bf16[32,16,192]{2,0,1:T(8,128)(2,1)S(1)}, u32[]{:S(2)}, u32[]{:S(2)}) async-start(bf16[32,16,192]{2,0,1:T(8,128)(2,1)} %copy.30), calls=%async_computation.1 | async-start | bytes 524288 | tf_op jit(solution)/shard_map/all_to_all | solution.py:28
  38.3 9.7 %all-to-all-done.1 = bf16[32,16,192]{2,0,1:T(8,128)(2,1)S(1)} async-done(((bf16[32,16,192]{2,0,1:T(8,128)(2,1)}), bf16[32,16,192]{2,0,1:T(8,128)(2,1)S(1)}, u32[]{:S(2)}, u32[]{:S(2)}) %all-to-all-start.1) | async-done | bytes 196640 | tf_op jit(solution)/shard_map/all_to_all | solution.py:28
  48.0 5.0 %all-to-all-start.2 = ((bf16[32,16,192]{2,0,1:T(8,128)(2,1)}), bf16[32,16,192]{2,0,1:T(8,128)(2,1)}, u32[]{:S(2)}, u32[]{:S(2)}) async-start(bf16[32,16,192]{2,0,1:T(8,128)(2,1)} %copy.57), calls=%async_computation.2 | async-start | bytes 524288 | tf_op jit(solution)/shard_map/all_to_all | solution.py:29
  53.3 1.3 collective-permute-start.7
  54.6 8.1 %collective-permute-start.6 = (bf16[512,192]{1,0:T(8,128)(2,1)S(1)}, bf16[512,192]{1,0:T(8,128)(2,1)}, u32[]{:S(2)}, u32[]{:S(2)}) collective-permute-start(bf16[512,192]{1,0:T(8,128)(2,1)S(1)} %bitcast.169), channel_id=1, source_target_pairs={{0,128},{16,144},{32,160},{48,176},{64,192},{80,208},{96,224},{112... | collective-permute-start | bytes 589832 | tf_op jit(solution)/shard_map/ppermute | solution.py:14
  62.7 1.3 collective-permute-start.5
  64.0 5.1 %collective-permute-start.4 = (bf16[512,192]{1,0:T(8,128)(2,1)S(1)}, bf16[512,192]{1,0:T(8,128)(2,1)S(1)}, u32[]{:S(2)}, u32[]{:S(2)}) collective-permute-start(bf16[512,192]{1,0:T(8,128)(2,1)S(1)} %bitcast.171), channel_id=1, source_target_pairs={{0,64},{16,80},{32,96},{48,112},{64,128},{80,144},{96,160},{112,17... | collective-permute-start | bytes 589832 | tf_op jit(solution)/shard_map/ppermute | solution.py:14
  69.1 1.3 collective-permute-start.3
  71.0 2.1 reshape.290
  73.9 2.4 fusion
  76.3 6.2 %collective-permute-start.2 = (bf16[512,192]{1,0:T(8,128)(2,1)S(1)}, bf16[512,192]{1,0:T(8,128)(2,1)}, u32[]{:S(2)}, u32[]{:S(2)}) collective-permute-start(bf16[512,192]{1,0:T(8,128)(2,1)S(1)} %bitcast.174), channel_id=1, source_target_pairs={{0,32},{16,48},{32,64},{48,80},{64,96},{80,112},{96,128},{112,144}... | collective-permute-start | bytes 589832 | tf_op jit(solution)/shard_map/ppermute | solution.py:14
  83.6 2.4 fusion.8
  86.0 1.3 collective-permute-start.1
  88.5 2.5 fusion.7
  91.7 4.7 %collective-permute-start = (bf16[512,192]{1,0:T(8,128)(2,1)S(1)}, bf16[512,192]{1,0:T(8,128)(2,1)}, u32[]{:S(2)}, u32[]{:S(2)}) collective-permute-start(bf16[512,192]{1,0:T(8,128)(2,1)S(1)} %bitcast.176), channel_id=1, source_target_pairs={{0,16},{16,32},{32,48},{48,64},{64,80},{80,96},{96,112},{112,128},... | collective-permute-start | bytes 589832 | tf_op jit(solution)/shard_map/ppermute | solution.py:14
  97.5 2.4 fusion.6
  100.0 1.3 collective-permute-start.9
  101.5 2.4 fusion.5
  103.9 5.5 %collective-permute-start.10 = (bf16[512,192]{1,0:T(8,128)(2,1)}, bf16[512,192]{1,0:T(8,128)(2,1)}, u32[]{:S(2)}, u32[]{:S(2)}) collective-permute-start(bf16[512,192]{1,0:T(8,128)(2,1)} %bitcast.31), channel_id=1, source_target_pairs={{0,32},{16,48},{32,64},{48,80},{64,96},{80,112},{96,128},{112,144}... | collective-permute-start | bytes 589832 | tf_op jit(solution)/shard_map/ppermute | solution.py:14
  109.6 2.4 fusion.4
  112.0 1.3 collective-permute-start.11
  114.5 2.4 fusion.3
  116.9 9.4 %collective-permute-start.12 = (bf16[512,192]{1,0:T(8,128)(2,1)}, bf16[512,192]{1,0:T(8,128)(2,1)}, u32[]{:S(2)}, u32[]{:S(2)}) collective-permute-start(bf16[512,192]{1,0:T(8,128)(2,1)} %bitcast.31), channel_id=1, source_target_pairs={{0,64},{16,80},{32,96},{48,112},{64,128},{80,144},{96,160},{112,17... | collective-permute-start | bytes 589832 | tf_op jit(solution)/shard_map/ppermute | solution.py:14
  126.3 1.8 copy.37
  128.1 3.4 %fusion.2 = (f32[3,512]{1,0:T(4,128)S(1)}, f32[3,512,512]{1,2,0:T(8,128)}) fusion(pred[512,512]{0,1:T(8,128)(4,1)S(1)} %bitcast.161, bf16[512,3,64]{0,2,1:T(8,128)(2,1)S(1)} %copy.31, bf16[512,3,64]{0,2,1:T(8,128)(2,1)} %bitcast.184), kind=kOutput, calls=%fused_computation.20 | convolution fusion | flops 103021056 | bytes 3807232 | tf_op jit(solution)/shard_map/qhd,khd->hqk/dot_general | solution.py:57
  131.5 1.5 collective-permute-start.13
  133.0 1.8 copy.34
  134.8 1.8 fusion.1
  136.8 12.5 %fusion.11 = (f32[3,512]{1,0:T(4,128)S(1)}, f32[3,512]{1,0:T(4,128)S(1)}, f32[3,512]{1,0:T(4,128)S(1)}, f32[3,512]{1,0:T(4,128)S(1)}, f32[3,512]{1,0:T(4,128)S(1...) fusion(f32[3,512,512]{1,2,0:T(8,128)S(1)} %get-tuple-element.40, ...), kind=kLoop, calls=%fused_computation.29 | loop fusion | flops 35375616 | bytes 30732288 | tf_op jit(solution)/shard_map/reduce_sum | solution.py:72
  149.3 1.8 fusion.27
  151.1 5.2 %collective-permute-start.14 = (bf16[512,192]{1,0:T(8,128)(2,1)}, bf16[512,192]{1,0:T(8,128)(2,1)}, u32[]{:S(2)}, u32[]{:S(2)}) collective-permute-start(bf16[512,192]{1,0:T(8,128)(2,1)} %bitcast.31), channel_id=1, source_target_pairs={{0,128},{16,144},{32,160},{48,176},{64,192},{80,208},{96,224},{112... | collective-permute-start | bytes 589832 | tf_op jit(solution)/shard_map/ppermute | solution.py:14
  157.3 3.6 %fusion.41 = f32[3,512,64]{1,2,0:T(8,128)} fusion(bf16[512,3,64]{0,2,1:T(8,128)(2,1)S(1)} %bitcast.186, f32[3,512,512]{1,2,0:T(8,128)} %get-tuple-element.36, f32[3,512]{1,0:T(4,128)S(1)} %maximum_maximum_fusion, pred[512,512]{0,1:T(8,128)(4,1)S(1)} %bitcast.163), kind=kOutput, calls=%fused_computation.52 | convolution fusion | flops 104595456 | bytes 4003840 | tf_op jit(solution)/shard_map/hqk,khd->qhd/dot_general | solution.py:73
  160.9 1.3 collective-permute-start.15
  163.3 3.6 %fusion.39 = f32[3,512,64]{1,2,0:T(8,128)} fusion(bf16[512,3,64]{0,2,1:T(8,128)(2,1)S(1)} %bitcast.187, f32[3,512,512]{1,2,0:T(8,128)} %get-tuple-element.34, f32[3,512]{1,0:T(4,128)S(1)} %maximum_maximum_fusion, pred[512,512]{0,1:T(8,128)(4,1)S(1)} %bitcast.160), kind=kOutput, calls=%fused_computation.51 | convolution fusion | flops 104595456 | bytes 4003840 | tf_op jit(solution)/shard_map/hqk,khd->qhd/dot_general | solution.py:73
  166.9 1.5 collective-permute-start.8
  169.5 3.6 %fusion.37 = f32[3,512,64]{1,2,0:T(8,128)} fusion(bf16[512,3,64]{0,2,1:T(8,128)(2,1)S(1)} %bitcast.188, f32[3,512,512]{1,2,0:T(8,128)} %get-tuple-element.32, f32[3,512]{1,0:T(4,128)S(1)} %maximum_maximum_fusion, pred[512,512]{0,1:T(8,128)(4,1)S(1)} %bitcast.157), kind=kOutput, calls=%fused_computation.50 | convolution fusion | flops 104595456 | bytes 4003840 | tf_op jit(solution)/shard_map/hqk,khd->qhd/dot_general | solution.py:73
  174.2 3.6 %fusion.35 = f32[3,512,64]{1,2,0:T(8,128)} fusion(bf16[512,3,64]{0,2,1:T(8,128)(2,1)S(1)} %bitcast.189, f32[3,512,512]{1,2,0:T(8,128)} %get-tuple-element.30, f32[3,512]{1,0:T(4,128)S(1)} %maximum_maximum_fusion, pred[512,512]{0,1:T(8,128)(4,1)S(1)} %bitcast.151), kind=kOutput, calls=%fused_computation.49 | convolution fusion | flops 104595456 | bytes 4003840 | tf_op jit(solution)/shard_map/hqk,khd->qhd/dot_general | solution.py:73
  178.9 3.6 %fusion.33 = f32[3,512,64]{1,2,0:T(8,128)} fusion(bf16[512,3,64]{0,2,1:T(8,128)(2,1)S(1)} %bitcast.190, f32[3,512,512]{1,2,0:T(8,128)} %get-tuple-element.28, f32[3,512]{1,0:T(4,128)S(1)} %maximum_maximum_fusion, pred[512,512]{0,1:T(8,128)(4,1)S(1)} %bitcast.148), kind=kOutput, calls=%fused_computation.48 | convolution fusion | flops 104595456 | bytes 4003840 | tf_op jit(solution)/shard_map/hqk,khd->qhd/dot_general | solution.py:73
  183.6 3.6 %fusion.31 = f32[3,512,64]{1,2,0:T(8,128)} fusion(bf16[512,3,64]{0,2,1:T(8,128)(2,1)S(1)} %bitcast.191, f32[3,512,512]{1,2,0:T(8,128)} %get-tuple-element.26, f32[3,512]{1,0:T(4,128)S(1)} %maximum_maximum_fusion, pred[512,512]{0,1:T(8,128)(4,1)S(1)} %bitcast.145), kind=kOutput, calls=%fused_computation.47 | convolution fusion | flops 104595456 | bytes 4003840 | tf_op jit(solution)/shard_map/hqk,khd->qhd/dot_general | solution.py:73
  187.4 3.7 %fusion.29 = f32[3,512,64]{1,2,0:T(8,128)} fusion(bf16[512,3,64]{0,2,1:T(8,128)(2,1)S(1)} %bitcast.192, f32[3,512,512]{1,2,0:T(8,128)} %get-tuple-element.24, f32[3,512]{1,0:T(4,128)S(1)} %maximum_maximum_fusion, pred[512,512]{0,1:T(8,128)(4,1)S(1)} %bitcast.142), kind=kOutput, calls=%fused_computation.46 | convolution fusion | flops 104595456 | bytes 4003840 | tf_op jit(solution)/shard_map/hqk,khd->qhd/dot_general | solution.py:73
  191.2 3.6 %fusion.84 = bf16[512,3,64]{0,2,1:T(8,128)(2,1)S(1)} fusion(f32[3,512,64]{1,2,0:T(8,128)} %fusion.29, f32[3,512,64]{1,2,0:T(8,128)} %fusion.31, f32[3,512,64]{1,2,0:T(8,128)} %fusion.33, f32[3,512,64]{1,2,0:T(8,128)} %fusion.35, f32[3,512,64]{1,2,0:T(8,128)} %fusion.37, f32[3,512,64]{1,2,0:T(8,128)} %fusion.39, f32[3,512,64]{1,2,0:T(8,128)S(1)} %copy-done.11, ...), kind=kOutput, calls=%fused_computation.73 | convolution fusion | flops 105578496 | bytes 6959104 | tf_op jit(solution)/shard_map/hqk,khd->qhd/dot_general | solution.py:73
  194.8 3.7 %fusion.126 = f32[512,3072]{1,0:T(8,128)} fusion(bf16[512,192]{0,1:T(8,128)(2,1)S(1)} %bitcast.193, bf16[192,3072]{1,0:T(8,128)(2,1)S(1)} %copy-done), kind=kOutput, calls=%fused_computation.143 | convolution fusion | flops 603979776 | bytes 7667712 | tf_op jit(solution)/shard_map/dot_general | solution.py:85
  199.2 126.6 %reduce-scatter.2.cloned.1.call-done = f32[32,3072]{1,0:T(8,128)} async-done(((f32[512,3072]{1,0:T(8,128)}), f32[32,3072]{1,0:T(8,128)}) %reduce-scatter.2.cloned.1.call-update) | async-done | bytes 393232 | tf_op jit(solution)/shard_map/reduce_scatter | solution.py:84
  325.8 1.7 add_convert_fusion
  (104 shorter events, 20.4 us)
Async XLA Ops:
  6.5 188.3 %copy-start = (bf16[192,3072]{1,0:T(8,128)(2,1)S(1)}, bf16[192,3072]{1,0:T(8,128)(2,1)}, u32[]{:S(2)}) copy-start(bf16[192,3072]{1,0:T(8,128)(2,1)} %param.10) | copy-start | bytes 3538948
  6.5 30.7 %copy-start.8 = (bf16[32,3072]{1,0:T(8,128)(2,1)S(1)}, bf16[32,3072]{1,0:T(8,128)(2,1)}, u32[]{:S(2)}) copy-start(bf16[32,3072]{1,0:T(8,128)(2,1)} %param.8) | copy-start | bytes 589828
  8.7 23.7 %all-to-all-start = ((bf16[32,16,192]{2,0,1:T(8,128)(2,1)}), bf16[32,16,192]{2,0,1:T(8,128)(2,1)S(1)}, u32[]{:S(2)}, u32[]{:S(2)}) async-start(bf16[32,16,192]{2,0,1:T(8,128)(2,1)} %copy.29), calls=%async_computation | async-start | bytes 524288 | tf_op jit(solution)/shard_map/all_to_all | solution.py:27
  32.4 15.6 %all-to-all-start.1 = ((bf16[32,16,192]{2,0,1:T(8,128)(2,1)}), bf16[32,16,192]{2,0,1:T(8,128)(2,1)S(1)}, u32[]{:S(2)}, u32[]{:S(2)}) async-start(bf16[32,16,192]{2,0,1:T(8,128)(2,1)} %copy.30), calls=%async_computation.1 | async-start | bytes 524288 | tf_op jit(solution)/shard_map/all_to_all | solution.py:28
  48.0 22.9 %all-to-all-start.2 = ((bf16[32,16,192]{2,0,1:T(8,128)(2,1)}), bf16[32,16,192]{2,0,1:T(8,128)(2,1)}, u32[]{:S(2)}, u32[]{:S(2)}) async-start(bf16[32,16,192]{2,0,1:T(8,128)(2,1)} %copy.57), calls=%async_computation.2 | async-start | bytes 524288 | tf_op jit(solution)/shard_map/all_to_all | solution.py:29
  53.0 272.8 %reduce-scatter.2.cloned.1.call-start = ((), (), s32[]{:S(2)}) async-start(), calls=%async_computation.4 | async-start | bytes 6684672 | tf_op jit(solution)/shard_map/reduce_scatter | solution.py:84
  53.3 22.9 %collective-permute-start.7 = (bf16[512,192]{1,0:T(8,128)(2,1)S(1)}, bf16[512,192]{1,0:T(8,128)(2,1)}, u32[]{:S(2)}, u32[]{:S(2)}) collective-permute-start(bf16[512,192]{1,0:T(8,128)(2,1)S(1)} %bitcast.168), channel_id=1, source_target_pairs={{128,0},{144,16},{160,32},{176,48},{192,64},{208,80},{224,96},{240... | collective-permute-start | bytes 589832 | tf_op jit(solution)/shard_map/ppermute | solution.py:14
  54.6 31.4 %collective-permute-start.6 = (bf16[512,192]{1,0:T(8,128)(2,1)S(1)}, bf16[512,192]{1,0:T(8,128)(2,1)}, u32[]{:S(2)}, u32[]{:S(2)}) collective-permute-start(bf16[512,192]{1,0:T(8,128)(2,1)S(1)} %bitcast.169), channel_id=1, source_target_pairs={{0,128},{16,144},{32,160},{48,176},{64,192},{80,208},{96,224},{112... | collective-permute-start | bytes 589832 | tf_op jit(solution)/shard_map/ppermute | solution.py:14
  62.7 28.3 %collective-permute-start.5 = (bf16[512,192]{1,0:T(8,128)(2,1)S(1)}, bf16[512,192]{1,0:T(8,128)(2,1)S(1)}, u32[]{:S(2)}, u32[]{:S(2)}) collective-permute-start(bf16[512,192]{1,0:T(8,128)(2,1)S(1)} %bitcast.170), channel_id=1, source_target_pairs={{64,0},{80,16},{96,32},{112,48},{128,64},{144,80},{160,96},{176,11... | collective-permute-start | bytes 589832 | tf_op jit(solution)/shard_map/ppermute | solution.py:14
  64.0 36.0 %collective-permute-start.4 = (bf16[512,192]{1,0:T(8,128)(2,1)S(1)}, bf16[512,192]{1,0:T(8,128)(2,1)S(1)}, u32[]{:S(2)}, u32[]{:S(2)}) collective-permute-start(bf16[512,192]{1,0:T(8,128)(2,1)S(1)} %bitcast.171), channel_id=1, source_target_pairs={{0,64},{16,80},{32,96},{48,112},{64,128},{80,144},{96,160},{112,17... | collective-permute-start | bytes 589832 | tf_op jit(solution)/shard_map/ppermute | solution.py:14
  69.1 34.8 %collective-permute-start.3 = (bf16[512,192]{1,0:T(8,128)(2,1)S(1)}, bf16[512,192]{1,0:T(8,128)(2,1)S(1)}, u32[]{:S(2)}, u32[]{:S(2)}) collective-permute-start(bf16[512,192]{1,0:T(8,128)(2,1)S(1)} %bitcast.172), channel_id=1, source_target_pairs={{32,0},{48,16},{64,32},{80,48},{96,64},{112,80},{128,96},{144,112}... | collective-permute-start | bytes 589832 | tf_op jit(solution)/shard_map/ppermute | solution.py:14
  73.1 0.7 copy-start.4
  76.3 35.8 %collective-permute-start.2 = (bf16[512,192]{1,0:T(8,128)(2,1)S(1)}, bf16[512,192]{1,0:T(8,128)(2,1)}, u32[]{:S(2)}, u32[]{:S(2)}) collective-permute-start(bf16[512,192]{1,0:T(8,128)(2,1)S(1)} %bitcast.174), channel_id=1, source_target_pairs={{0,32},{16,48},{32,64},{48,80},{64,96},{80,112},{96,128},{112,144}... | collective-permute-start | bytes 589832 | tf_op jit(solution)/shard_map/ppermute | solution.py:14
  86.0 30.9 %collective-permute-start.1 = (bf16[512,192]{1,0:T(8,128)(2,1)S(1)}, bf16[512,192]{1,0:T(8,128)(2,1)}, u32[]{:S(2)}, u32[]{:S(2)}) collective-permute-start(bf16[512,192]{1,0:T(8,128)(2,1)S(1)} %bitcast.175), channel_id=1, source_target_pairs={{16,0},{32,16},{48,32},{64,48},{80,64},{96,80},{112,96},{128,112},... | collective-permute-start | bytes 589832 | tf_op jit(solution)/shard_map/ppermute | solution.py:14
  90.9 0.7 copy-start.7
  91.7 39.9 %collective-permute-start = (bf16[512,192]{1,0:T(8,128)(2,1)S(1)}, bf16[512,192]{1,0:T(8,128)(2,1)}, u32[]{:S(2)}, u32[]{:S(2)}) collective-permute-start(bf16[512,192]{1,0:T(8,128)(2,1)S(1)} %bitcast.176), channel_id=1, source_target_pairs={{0,16},{16,32},{32,48},{48,64},{64,80},{80,96},{96,112},{112,128},... | collective-permute-start | bytes 589832 | tf_op jit(solution)/shard_map/ppermute | solution.py:14
  100.0 51.1 %collective-permute-start.9 = (bf16[512,192]{1,0:T(8,128)(2,1)}, bf16[512,192]{1,0:T(8,128)(2,1)}, u32[]{:S(2)}, u32[]{:S(2)}) collective-permute-start(bf16[512,192]{1,0:T(8,128)(2,1)} %bitcast.31), channel_id=1, source_target_pairs={{16,0},{32,16},{48,32},{64,48},{80,64},{96,80},{112,96},{128,112},... | collective-permute-start | bytes 589832 | tf_op jit(solution)/shard_map/ppermute | solution.py:14
  103.9 57.0 %collective-permute-start.10 = (bf16[512,192]{1,0:T(8,128)(2,1)}, bf16[512,192]{1,0:T(8,128)(2,1)}, u32[]{:S(2)}, u32[]{:S(2)}) collective-permute-start(bf16[512,192]{1,0:T(8,128)(2,1)} %bitcast.31), channel_id=1, source_target_pairs={{0,32},{16,48},{32,64},{48,80},{64,96},{80,112},{96,128},{112,144}... | collective-permute-start | bytes 589832 | tf_op jit(solution)/shard_map/ppermute | solution.py:14
  112.0 54.9 %collective-permute-start.11 = (bf16[512,192]{1,0:T(8,128)(2,1)}, bf16[512,192]{1,0:T(8,128)(2,1)}, u32[]{:S(2)}, u32[]{:S(2)}) collective-permute-start(bf16[512,192]{1,0:T(8,128)(2,1)} %bitcast.31), channel_id=1, source_target_pairs={{32,0},{48,16},{64,32},{80,48},{96,64},{112,80},{128,96},{144,112}... | collective-permute-start | bytes 589832 | tf_op jit(solution)/shard_map/ppermute | solution.py:14
  116.9 56.2 %collective-permute-start.12 = (bf16[512,192]{1,0:T(8,128)(2,1)}, bf16[512,192]{1,0:T(8,128)(2,1)}, u32[]{:S(2)}, u32[]{:S(2)}) collective-permute-start(bf16[512,192]{1,0:T(8,128)(2,1)} %bitcast.31), channel_id=1, source_target_pairs={{0,64},{16,80},{32,96},{48,112},{64,128},{80,144},{96,160},{112,17... | collective-permute-start | bytes 589832 | tf_op jit(solution)/shard_map/ppermute | solution.py:14
  131.5 46.3 %collective-permute-start.13 = (bf16[512,192]{1,0:T(8,128)(2,1)}, bf16[512,192]{1,0:T(8,128)(2,1)}, u32[]{:S(2)}, u32[]{:S(2)}) collective-permute-start(bf16[512,192]{1,0:T(8,128)(2,1)} %bitcast.31), channel_id=1, source_target_pairs={{64,0},{80,16},{96,32},{112,48},{128,64},{144,80},{160,96},{176,11... | collective-permute-start | bytes 589832 | tf_op jit(solution)/shard_map/ppermute | solution.py:14
  134.8 2.0 copy-start.1
  136.7 12.6 %copy-start.2 = (f32[3,512,512]{1,2,0:T(8,128)}, f32[3,512,512]{1,2,0:T(8,128)S(1)}, u32[]{:S(2)}) copy-start(f32[3,512,512]{1,2,0:T(8,128)S(1)} %get-tuple-element.40) | copy-start | bytes 9437188
  136.7 12.5 %copy-start.3 = (f32[3,512,512]{1,2,0:T(8,128)S(1)}, f32[3,512,512]{1,2,0:T(8,128)}, u32[]{:S(2)}) copy-start(f32[3,512,512]{1,2,0:T(8,128)} %get-tuple-element.38) | copy-start | bytes 9437188
  136.7 12.5 %copy-start.5 = (pred[512,4,128]{0,2,1:T(8,128)(4,1)S(1)}, pred[512,4,128]{0,2,1:T(8,128)(4,1)}, u32[]{:S(2)}) copy-start(pred[512,4,128]{0,2,1:T(8,128)(4,1)} %copy-done.4) | copy-start | bytes 786436
  136.7 12.5 %copy-start.6 = (bf16[512,3,64]{2,1,0:T(4,128)(2,1)S(1)}, bf16[512,3,64]{2,1,0:T(4,128)(2,1)}, u32[]{:S(2)}) copy-start(bf16[512,3,64]{2,1,0:T(4,128)(2,1)} %reshape.290) | copy-start | bytes 589828
  151.1 31.4 %collective-permute-start.14 = (bf16[512,192]{1,0:T(8,128)(2,1)}, bf16[512,192]{1,0:T(8,128)(2,1)}, u32[]{:S(2)}, u32[]{:S(2)}) collective-permute-start(bf16[512,192]{1,0:T(8,128)(2,1)} %bitcast.31), channel_id=1, source_target_pairs={{0,128},{16,144},{32,160},{48,176},{64,192},{80,208},{96,224},{112... | collective-permute-start | bytes 589832 | tf_op jit(solution)/shard_map/ppermute | solution.py:14
  160.9 26.3 %collective-permute-start.15 = (bf16[512,192]{1,0:T(8,128)(2,1)}, bf16[512,192]{1,0:T(8,128)(2,1)S(1)}, u32[]{:S(2)}, u32[]{:S(2)}) collective-permute-start(bf16[512,192]{1,0:T(8,128)(2,1)} %bitcast.31), channel_id=1, source_target_pairs={{128,0},{144,16},{160,32},{176,48},{192,64},{208,80},{224,96},{240... | collective-permute-start | bytes 589832 | tf_op jit(solution)/shard_map/ppermute | solution.py:14
  166.9 24.1 %collective-permute-start.8 = (bf16[512,192]{1,0:T(8,128)(2,1)}, bf16[512,192]{1,0:T(8,128)(2,1)S(1)}, u32[]{:S(2)}, u32[]{:S(2)}) collective-permute-start(bf16[512,192]{1,0:T(8,128)(2,1)} %bitcast.31), channel_id=1, source_target_pairs={{0,16},{16,32},{32,48},{48,64},{64,80},{80,96},{96,112},{112,128},... | collective-permute-start | bytes 589832 | tf_op jit(solution)/shard_map/ppermute | solution.py:14
  187.3 3.9 %copy-start.10 = (f32[3,512,64]{1,2,0:T(8,128)S(1)}, f32[3,512,64]{1,2,0:T(8,128)}, u32[]{:S(2)}) copy-start(f32[3,512,64]{1,2,0:T(8,128)} %fusion.27) | copy-start | bytes 1179652
  187.3 3.9 %copy-start.11 = (f32[3,512,64]{1,2,0:T(8,128)S(1)}, f32[3,512,64]{1,2,0:T(8,128)}, u32[]{:S(2)}) copy-start(f32[3,512,64]{1,2,0:T(8,128)} %fusion.41) | copy-start | bytes 1179652
  198.5 0.7 copy-start.9
Sparse Core Ops, SparseCore 0:
  198.6 127.0 reduce-scatter.1
where the time goes:
time: 336 us; the launch traced here: 334 us
  waiting for transfers between devices  143 us (43%)
  starting transfers between devices  78 us (23%)
  matrix products  56.6 us (17%)
  local copies, waits for them, and re-layouts  27.3 us (8%)
  other arithmetic  15.4 us (5%)
  between operations  13.9 us (4%)
    reduce_scatter x1, waiting for transfers between devices, shards(): lax.psum_scatter(jnp.dot(attended, out_weight, preferred_element_type=jnp...  127 us
    ppermute x16, starting transfers between devices, shifted(): lax.ppermute(value, axis, [(source, source + steps) for source in range(f...  56.1 us
    dot_general x9, matrix products, shards(): jnp.einsum('hqk,khd->qhd', weights.astype(jnp.bfloat16), values_here, pre...  30.7 us
    dot_general x9, matrix products, shards(): jnp.einsum('qhd,khd->hqk', queries, keys_here.reshape(tok_rows, head_coun...  22.3 us
    ppermute x16, local copies, waits for them, and re-layouts, shifted(): lax.ppermute(value, axis, [(source, source + steps) for source in range(f...  14.7 us
    all_to_all x1, starting transfers between devices, shards(): lax.all_to_all(query_in, 'head', split_axis=1, concat_axis=0, tiled=True)  12.6 us
    reduce_sum x1, other arithmetic, shards(): total = total + jnp.sum(weights, axis=2)  12.5 us
    all_to_all x1, waiting for transfers between devices, shards(): lax.all_to_all(key_in, 'head', split_axis=1, concat_axis=0, tiled=True)  9.74 us
  transfers between devices with their start and end apart: 20, of which 3 were waited for; matrix products, arithmetic and copies ran while one was open for 25% of the time, Pallas kernels for 0%

commit v1 on v0

v1 whole, which is shorter than its diff:
```python
import math

import jax
import jax.numpy as jnp
from jax import lax
from jax.experimental import pallas as pl
from jax.experimental.pallas import tpu as pltpu
from jax.sharding import PartitionSpec as P

MESH = pl.DeviceIdType.MESH
F32 = jnp.float32
BF16 = jnp.bfloat16
HD = 64
NEG = -1e30
SCALE2 = math.log2(math.e) / math.sqrt(HD)


def kernel(
    q_ref, k_ref, v_ref, mask, w_hbm, bias_ref, o_ref,
    sendbuf, recv, kvall, qp, m_ref, l_ref, acc_ref, opack, orecv, ag, wbuf, part, dpart, fin,
    e_send, e_recv, x_send, x_recv, f_send, f_recv,
    w1_send, w1_recv, w1_loc, w2_send, w2_recv, w2f_send, w3_send, w3_recv, w3f_send, w3f_recv,
    o_send, o_recv, a_send, a_recv, af_send, af_recv, d_send, d_recv, y_send, y_recv,
):
    seq = lax.axis_index("seq")
    g = lax.axis_index("head")
    a_me, x = seq // 4, seq % 4
    zh, y, c = g // 8, (g // 2) % 4, g % 2
    k_me = (a_me + 3 - y) % 4
    active = k_me < 3
    boundary = (a_me % 3) == 0

    def remote(src, dst, send, rcv, dev):
        return pltpu.make_async_remote_copy(
            src_ref=src, dst_ref=dst, send_sem=send, recv_sem=rcv, device_id=dev, device_id_type=MESH
        )

    def arrived(dst, sem):
        pltpu.make_async_copy(dst, dst, sem).wait()

    lane = lax.broadcasted_iota(jnp.int32, (32, 128), 1) < HD
    lane16 = lax.broadcasted_iota(jnp.int32, (16, 128), 1) < HD

    def head_device(h):
        gd, kd = h // 3, h % 3
        ad = ((gd // 2) % 4 + 1 + kd) % 4
        return ad, gd

    def prepare(p, carry):
        cols = pl.ds(pl.multiple_of(p * 128, 128), 128)
        k2 = k_ref[:, cols].astype(F32)
        v2 = v_ref[:, cols].astype(F32)
        q2 = q_ref[:, cols].astype(F32)
        kr, vr = pltpu.roll(k2, HD, 1), pltpu.roll(v2, HD, 1)
        qr = pltpu.roll(q2, HD, 1)
        sendbuf[2 * p, 0:32] = jnp.where(lane, k2, vr).astype(BF16)
        sendbuf[2 * p, 32:48] = jnp.where(lane16, q2[0:16], qr[16:32]).astype(BF16)
        sendbuf[2 * p + 1, 0:32] = jnp.where(lane, kr, v2).astype(BF16)
        sendbuf[2 * p + 1, 32:48] = jnp.where(lane16, qr[0:16], q2[16:32]).astype(BF16)
        return carry

    lax.fori_loop(0, 24, prepare, 0)

    def send_one(n, carry):
        h = (n + 3 * g) % 48
        ad, gd = head_device(h)
        here = (ad == a_me) & (gd == g)

        @pl.when(jnp.logical_not(here))
        def _():
            remote(
                sendbuf.at[h], recv.at[a_me, g], e_send, e_recv.at[a_me], (ad * 4 + x, gd)
            ).start()

        @pl.when(here)
        def _():
            pltpu.make_async_copy(sendbuf.at[h], recv.at[a_me, g], e_recv.at[a_me]).start()

        return carry

    lax.fori_loop(0, 48, send_one, 0)

    def wcols(yy):
        return w_hbm.at[:, pl.ds(pl.multiple_of(yy * 768, 128), 768)]

    w1 = []
    for r in range(1, 4):
        yd = (y + r) % 4
        cp = remote(
            wcols(yd), wbuf.at[y, zh], w1_send.at[r - 1], w1_recv.at[r - 1], (seq, zh * 8 + yd * 2 + c)
        )
        cp.start()
        w1.append(cp)
    w1_own = pltpu.make_async_copy(wcols(y), wbuf.at[y, zh], w1_loc)
    w1_own.start()

    right = (a_me * 4 + (x + 1) % 4, g)
    left = (a_me * 4 + (x + 3) % 4, g)
    lane64 = lax.broadcasted_iota(jnp.int32, (256, 128), 1) < HD

    def x_copy(direction, a):
        dev = right if direction == 0 else left
        return remote(
            kvall.at[0, a], kvall.at[1 + direction, a],
            x_send.at[direction, a], x_recv.at[direction, a], dev,
        )

    def f_copy(a):
        if a < 2:
            return remote(kvall.at[1, a], kvall.at[3, a], f_send.at[a], f_recv.at[a], right)
        return remote(kvall.at[2, a], kvall.at[3, a], f_send.at[a], f_recv.at[a], left)

    @pl.when(active)
    def _():
        for a in (0, 2, 1, 3):
            arrived(recv.at[a], e_recv.at[a])
            kvall[0, a] = recv[a, :, 0:32, :].reshape(512, 128)
            x_copy(0, a).start()
            x_copy(1, a).start()
            qx = recv[a, :, 32:48, :].astype(F32).reshape(256, 128)
            lo = jnp.where(lane64, qx, 0.0).astype(BF16)
            hi = jnp.where(lane64, pltpu.roll(qx, HD, 1), 0.0).astype(BF16)
            qp[a, :, 0:64, :] = lo.reshape(4, 64, 128)
            qp[a, :, 64:128, :] = hi.reshape(4, 64, 128)
            m_ref[a] = jnp.full((4, 128, 128), NEG, F32)
            l_ref[a] = jnp.zeros((4, 128, 128), F32)
            acc_ref[a] = jnp.zeros((4, 128, 128), F32)

    for cp in w1:
        cp.wait()
    w1_own.wait()
    other = 1 - zh
    w2 = remote(
        wbuf.at[x, zh], wbuf.at[x, zh], w2_send, w2_recv, ((3 - a_me) * 4 + x, other * 8 + y * 2 + c)
    )
    w2f = remote(
        wbuf.at[x, other], wbuf.at[x, other], w2f_send, w2_recv, ((1 + a_me // 3) * 4 + x, g)
    )

    @pl.when(boundary)
    def _():
        w2.start()

    def attend(buf, ap, a, midx):
        kv = kvall[buf, ap]
        for i in range(4):
            s = lax.dot_general(
                qp[a, i], kv, (((1,), (1,)), ((), ())), preferred_element_type=F32
            )
            cols = []
            for j in range(4):
                bias = jnp.where(mask[midx, i, j] > 0, 0.0, NEG).astype(F32)
                cols.append(s[:, j * 128:(j + 1) * 128] + bias)
            top = jnp.maximum(jnp.maximum(cols[0], cols[1]), jnp.maximum(cols[2], cols[3]))
            m_old = m_ref[a, i]
            m_new = jnp.maximum(m_old, jnp.max(top, axis=1, keepdims=True))
            alpha = jnp.exp2((m_old - m_new) * SCALE2)
            ps = [jnp.exp2((col - m_new) * SCALE2) for col in cols]
            l_ref[a, i] = l_ref[a, i] * alpha + ((ps[0] + ps[1]) + (ps[2] + ps[3]))
            p = jnp.concatenate([w.astype(BF16) for w in ps], axis=1)
            acc_ref[a, i] = acc_ref[a, i] * alpha + jnp.dot(p, kv, preferred_element_type=F32)
            m_ref[a, i] = m_new

    def local_round(d):
        def body(a, carry):
            ap = (a + d) % 4
            off = ap - a

            @pl.when((off <= 2) & (off >= -2))
            def _():
                if d == 0:
                    midx = 0
                else:
                    midx = jnp.where(off > 0, 4 + 2 * off, 3 - 2 * off)
                attend(0, ap, a, midx)

            return carry

        lax.fori_loop(0, 4, body, 0)

    def got_x(direction, a):
        x_copy(direction, a).wait_recv()

    @pl.when(active)
    def _():
        local_round(0)
        got_x(0, 0)
        f_copy(0).start()
        got_x(1, 2)
        f_copy(2).start()
        local_round(1)
        got_x(0, 1)
        f_copy(1).start()
        got_x(1, 3)
        f_copy(3).start()

    w3r = remote(
        wbuf.at[x, other], wbuf.at[x, other], w3_send.at[0], w3_recv.at[0], right
    )
    w3l = remote(
        wbuf.at[x, other], wbuf.at[x, other], w3_send.at[1], w3_recv.at[1], left
    )

    @pl.when(boundary)
    def _():
        w2.wait_recv()
        w2f.start()
        w3r.start()
        w3l.start()

    @pl.when(active)
    def _():
        local_round(2)
        local_round(3)
        for a in range(2, 4):
            got_x(0, a)
            got_x(1, 3 - a)

        def near(ap, carry):
            a_minus = ap + (3 - x) // 3
            a_plus = ap - (x + 1) // 4

            @pl.when(a_minus < 4)
            def _():
                attend(1, ap, a_minus, 1)

            @pl.when(a_plus >= 0)
            def _():
                attend(2, ap, a_plus, 2)

            return carry

        lax.fori_loop(0, 4, near, 0)

    @pl.when(jnp.logical_not(boundary))
    def _():
        w2.wait_recv()
        w3r.start()
        w3l.start()

    lane_o = lax.broadcasted_iota(jnp.int32, (64, 128), 1) < HD

    @pl.when(active)
    def _():
        for a in range(4):
            f_copy(a).wait_recv()

        def far(ap, carry):
            a_minus = ap + (3 - x) // 2
            a_plus = ap - (x + 2) // 4

            @pl.when(a_minus < 4)
            def _():
                attend(3, ap, a_minus, 3)

            @pl.when(a_plus >= 0)
            def _():
                attend(3, ap, a_plus, 4)

            return carry

        lax.fori_loop(0, 4, far, 0)

        def finish(n, carry):
            a, i = n // 4, n % 4
            total = jnp.sum(l_ref[a, i], axis=1, keepdims=True)
            att = acc_ref[a, i] / total
            packed = jnp.where(lane_o, pltpu.roll(att[0:64], HD, 1), att[64:128]).astype(BF16)
            opack[n // 2, n % 2] = packed
            return carry

        lax.fori_loop(0, 16, finish, 0)

        for n in range(8):
            ad, hd = n // 2, n % 2
            slot = zh * 3 + k_me
            here = (a_me == ad) & (zh == hd)
            src = opack.at[n]

            @pl.when(jnp.logical_not(here))
            def _():
                remote(
                    src, orecv.at[slot], o_send, o_recv, (ad * 4 + x, hd * 8 + y * 2 + c)
                ).start()

            @pl.when(here)
            def _():
                pltpu.make_async_copy(src, orecv.at[slot], o_recv).start()

    arrived(orecv, o_recv)
    lane_a = lax.broadcasted_iota(jnp.int32, (128, 128), 1) < HD
    for t in range(3):
        x0 = orecv[2 * t].astype(F32).reshape(128, 128)
        x1 = orecv[2 * t + 1].astype(F32).reshape(128, 128)
        cols = slice(t * 128, (t + 1) * 128)
        ag[0, 0, :, cols] = jnp.where(lane_a, x0, pltpu.roll(x1, HD, 1)).astype(BF16)
        ag[0, 1, :, cols] = jnp.where(lane_a, pltpu.roll(x0, HD, 1), x1).astype(BF16)
    ynext = (seq, zh * 8 + ((y + 1) % 4) * 2 + c)
    yprev = (seq, zh * 8 + ((y + 3) % 4) * 2 + c)
    ar = remote(ag.at[0], ag.at[1], a_send.at[0], a_recv.at[0], ynext)
    al = remote(ag.at[0], ag.at[2], a_send.at[1], a_recv.at[1], yprev)
    ar.start()
    al.start()

    xl, xr = (x + 3) % 4, (x + 1) % 4
    w3r.wait_recv()
    src_l = wbuf.at[xl, other, pl.ds(0, 96)]
    w3fr = remote(src_l, src_l, w3f_send.at[0], w3f_recv.at[0], right)
    w3fr.start()
    w3l.wait_recv()
    src_r = wbuf.at[xr, other, pl.ds(96, 96)]
    w3fl = remote(src_r, src_r, w3f_send.at[1], w3f_recv.at[1], left)
    w3fl.start()

    ar.wait_recv()
    afr = remote(ag.at[1, 0], ag.at[3, 0], af_send.at[0], af_recv.at[0], ynext)
    afr.start()
    al.wait_recv()
    afl = remote(ag.at[2, 1], ag.at[3, 1], af_send.at[1], af_recv.at[1], yprev)
    afl.start()
    w3fr.wait_recv()
    w3fl.wait_recv()

    def project(slot, yy, first):
        lhs = ag[slot].reshape(256, 384)
        for n in range(3):
            cols = slice(n * 256, (n + 1) * 256)
            res = jnp.dot(
                lhs, wbuf[yy, :, :, cols].reshape(384, 256), preferred_element_type=F32
            ).reshape(2, 4, 2, 16, 256)
            if first:
                part[:, :, :, :, cols] = res
            else:
                part[:, :, :, :, cols] += res

    project(0, y, True)
    project(1, (y + 3) % 4, False)
    project(2, (y + 1) % 4, False)
    afr.wait_recv()
    afl.wait_recv()
    project(3, (y + 2) % 4, False)

    dcp = remote(part.at[:, :, 1 - c], dpart, d_send, d_recv, (seq, g + 1 - 2 * c))
    dcp.start()
    dcp.wait_recv()
    my_cols = pl.ds(pl.multiple_of(y * 768, 128), 768)
    bias = bias_ref[:, my_cols].astype(F32)
    for yd in range(4):
        for half in range(2):
            fin[yd, pl.ds(16 * half, 16), :] = (part[half, yd, c] + dpart[half, yd] + bias).astype(BF16)
    ys = []
    for r in range(1, 4):
        yd = (y + r) % 4
        cp = remote(
            fin.at[yd], o_ref.at[:, my_cols], y_send.at[r - 1], y_recv.at[r - 1], (seq, zh * 8 + yd * 2 + c)
        )
        cp.start()
        ys.append(cp)
    o_ref[:, my_cols] = fin[y]

    @pl.when(active)
    def _():
        arrived(sendbuf.at[pl.ds(0, 47)], e_send)
        for a in range(4):
            x_copy(0, a).wait_send()
            x_copy(1, a).wait_send()
            f_copy(a).wait_send()
        arrived(opack.at[pl.ds(0, 7)], o_send)

    @pl.when(jnp.logical_not(active))
    def _():
        arrived(sendbuf, e_send)

    @pl.when(boundary)
    def _():
        w2.wait_send()
        w2f.wait_send()

    for cp in (w3r, w3l, w3fr, w3fl, ar, al, afr, afl, dcp):
        cp.wait_send()
    for cp in ys:
        cp.wait()


def shards(query_in, key_in, value_in, block_mask, out_weight, out_bias):
    vmem = pl.BlockSpec(memory_space=pltpu.VMEM)
    dma = pltpu.SemaphoreType.DMA
    return pl.pallas_call(
        kernel,
        out_shape=jax.ShapeDtypeStruct((32, 3072), BF16),
        in_specs=[
            vmem, vmem, vmem,
            pl.BlockSpec(memory_space=pltpu.SMEM),
            pl.BlockSpec(memory_space=pl.ANY),
            vmem,
        ],
        out_specs=vmem,
        scratch_shapes=[
            pltpu.VMEM((48, 48, 128), BF16),
            pltpu.VMEM((4, 16, 48, 128), BF16),
            pltpu.VMEM((4, 4, 512, 128), BF16),
            pltpu.VMEM((4, 4, 128, 128), BF16),
            pltpu.VMEM((4, 4, 128, 128), F32),
            pltpu.VMEM((4, 4, 128, 128), F32),
            pltpu.VMEM((4, 4, 128, 128), F32),
            pltpu.VMEM((8, 2, 64, 128), BF16),
            pltpu.VMEM((6, 2, 64, 128), BF16),
            pltpu.VMEM((4, 2, 128, 384), BF16),
            pltpu.VMEM((4, 2, 192, 768), BF16),
            pltpu.VMEM((2, 4, 2, 16, 768), F32),
            pltpu.VMEM((2, 4, 16, 768), F32),
            pltpu.VMEM((4, 32, 768), BF16),
            dma, dma((4,)), dma((2, 4)), dma((2, 4)), dma((4,)), dma((4,)),
            dma((3,)), dma((3,)), dma, dma, dma, dma, dma((2,)), dma((2,)), dma((2,)), dma((2,)),
            dma, dma, dma((2,)), dma((2,)), dma((2,)), dma((2,)), dma, dma, dma((3,)), dma((3,)),
        ],
        compiler_params=pltpu.CompilerParams(
            has_side_effects=True, vmem_limit_bytes=40 * 1024 * 1024
        ),
        name="radial",
    )(query_in, key_in, value_in, block_mask, out_weight, out_bias.reshape(1, 3072))


def solution(mesh):
    return jax.shard_map(
        shards,
        mesh=mesh,
        in_specs=(
            P(("seq", "head"), None),
            P(("seq", "head"), None),
            P(("seq", "head"), None),
            P(),
            P("head", None),
            P(),
        ),
        out_specs=P(("seq", "head"), None),
        check_vma=False,
    )
```

time: 336 us -> 113 us (0.34)
  waiting for transfers between devices: 143 us -> 0 us
  Pallas kernels: 0 us -> 105 us
  starting transfers between devices: 78 us -> 0 us
  matrix products: 56.6 us -> 0 us
  local copies, waits for them, and re-layouts: 27.3 us -> 6.23 us
  other arithmetic: 15.4 us -> 0 us
  between operations: 13.9 us -> 0.01 us
    reduce_scatter x1 -> x0, waiting for transfers between devices: 127 us -> none  [shards(): lax.psum_scatter(jnp.dot(attended, out_weight, preferred_element_type=jnp...]
    pallas_call x0 -> x1, Pallas kernels: none -> 105 us  [shards(): pl.pallas_call(kernel, out_shape=jax.ShapeDtypeStruct((32, 3072), BF16),...]
    dot_general x19 -> x0, matrix products: 56.6 us -> none  [the longest x9 30.7 us: shards(): jnp.einsum('hqk,khd->qhd', weights.astype(jnp.bfloat16), values_here, pre...]
    ppermute x16 -> x0, starting transfers between devices: 56.1 us -> none  [shifted(): lax.ppermute(value, axis, [(source, source + steps) for source in range(f...]
    all_to_all x3 -> x0, starting transfers between devices: 22 us -> none  [the longest x1 12.6 us: shards(): lax.all_to_all(query_in, 'head', split_axis=1, concat_axis=0, tiled=True)]
    all_to_all x3 -> x0, waiting for transfers between devices: 16.5 us -> none  [the longest x1 9.74 us: shards(): lax.all_to_all(key_in, 'head', split_axis=1, concat_axis=0, tiled=True)]
    ppermute x16 -> x0, local copies, waits for them, and re-layouts: 14.7 us -> none  [shifted(): lax.ppermute(value, axis, [(source, source + steps) for source in range(f...]
    reduce_sum x1 -> x0, other arithmetic: 12.5 us -> none  [shards(): total = total + jnp.sum(weights, axis=2)]
  transfers between devices with their start and end apart: 20 -> 0, of which waited for: 3 -> 0; matrix products, arithmetic and copies ran while one was open for 25% -> 0% of each run, Pallas kernels for 0% -> 0%
where the time goes in v1:
time: 113 us; the launch traced here: 111 us
  Pallas kernels  105 us (93%)
  local copies, waits for them, and re-layouts  6.23 us (6%)
    pallas_call x1, Pallas kernels, shards(): pl.pallas_call(kernel, out_shape=jax.ShapeDtypeStruct((32, 3072), BF16),...  105 us
    unnamed x10, local copies, waits for them, and re-layouts  5.53 us

profile of v1, /device:TPU:1, one launch (start us, length us, event | category | flops | bytes accessed | tf_op | source)
XLA Modules:
  0.0 111.4 jit_solution(5871309279399237434)
XLA Ops:
  0.0 0.7 reshape.3.bias_ref
  0.7 0.8 copy.7.mask
  1.5 0.0 copy-start
  1.5 1.3 %copy-done = bf16[192,3072]{1,0:T(8,128)(2,1)S(1)} copy-done((bf16[192,3072]{1,0:T(8,128)(2,1)S(1)}, bf16[192,3072]{1,0:T(8,128)(2,1)}, u32[]{:S(2)}) %copy-start) | copy-done | bytes 1179672
  2.8 0.0 copy-start.1
  2.8 0.9 copy-done.1
  3.7 0.0 copy-start.2
  3.7 0.9 copy-done.2
  4.6 0.0 copy-start.3
  4.6 0.9 copy-done.3
  5.6 105.1 %radial.1 = bf16[32,3072]{1,0:T(8,128)(2,1)S(1)} custom-call(bf16[32,3072]{1,0:T(8,128)(2,1)S(1)} %copy-done.1, bf16[32,3072]{1,0:T(8,128)(2,1)S(1)} %copy-done.2, bf16[32,3072]{1,0:T(8,128)(2,1)S(1)} %copy-done.3, s32[9,4,4]{2,1,0:T(4,128)S(1)} %copy.7.mask, bf16[192,3072]{1,0:T(8,128)(2,1)S(1)} %copy-done, bf16[1,3072]{1,0:T(2,128)(2,1)S(1)} %reshape.3.bias_ref), custom_call_target="tpu_custom_call" | custom-call | tf_op jit(solution)/shard_map/radial/pallas_call | solution.py:388
  110.7 0.7 copy.9
Async XLA Ops:
  1.5 1.3 %copy-start = (bf16[192,3072]{1,0:T(8,128)(2,1)S(1)}, bf16[192,3072]{1,0:T(8,128)(2,1)}, u32[]{:S(2)}) copy-start(bf16[192,3072]{1,0:T(8,128)(2,1)} %w_hbm.1) | copy-start | bytes 3538948
  2.8 0.9 copy-start.1
  3.7 0.9 copy-start.2
  4.6 0.9 copy-start.3

commit v2 on v0

v2 whole, which is shorter than its diff:
```python
import functools
import math

import jax
import jax.numpy as jnp
from jax import lax
from jax.experimental import pallas as pl
from jax.experimental.pallas import tpu as pltpu
from jax.sharding import PartitionSpec as P

MESH = pl.DeviceIdType.MESH
F32 = jnp.float32
BF16 = jnp.bfloat16
HD = 64
NEG = -1e30
SCALE2 = math.log2(math.e) / math.sqrt(HD)
SLOTS = (0, 3, 1, 4, 2, 5)


def kernel(
    q_hbm, k_hbm, v_hbm, mask_hbm, w_hbm, bias_hbm, o_ref,
    raw, mask, bias_ref, sendbuf, kbuf, vbuf, qbuf, qlo, qhi, tiles, m_ref, l_ref, acc_ref, opack,
    attended, lhs, wbuf, part, dpart, fin,
    in_sem, e_send, e_recv, x_send, x_recv, f_send, f_recv,
    w1_send, w1_recv, w1_loc, w2_send, w2_recv, w2f_send, w3_send, w3_recv, w3f_send, w3f_recv,
    o_send, o_recv, a_send, a_recv, af_send, af_recv, d_send, d_recv, y_send, y_recv,
):
    seq = lax.axis_index("seq")
    g = lax.axis_index("head")
    a_me, x = seq // 4, seq % 4
    zh, y, c = g // 8, (g // 2) % 4, g % 2
    k_me = (a_me + 3 - y) % 4
    active = k_me < 3
    boundary = (a_me % 3) == 0
    right = (a_me * 4 + (x + 1) % 4, g)
    left = (a_me * 4 + (x + 3) % 4, g)
    ynext = (seq, zh * 8 + ((y + 1) % 4) * 2 + c)
    yprev = (seq, zh * 8 + ((y + 3) % 4) * 2 + c)
    other = 1 - zh

    def remote(src, dst, send, rcv, dev):
        return pltpu.make_async_remote_copy(
            src_ref=src, dst_ref=dst, send_sem=send, recv_sem=rcv, device_id=dev, device_id_type=MESH
        )

    def arrived(dst, sem):
        pltpu.make_async_copy(dst, dst, sem).wait()

    fetch = [
        pltpu.make_async_copy(src, raw.at[n], in_sem.at[n]) for n, src in enumerate((k_hbm, v_hbm, q_hbm))
    ]
    fetch.append(pltpu.make_async_copy(bias_hbm, bias_ref, in_sem.at[3]))
    fetch.append(pltpu.make_async_copy(mask_hbm, mask, in_sem.at[4]))
    for cp in fetch:
        cp.start()
    barrier = pltpu.get_barrier_semaphore()
    for n in range(1, 64):
        pl.semaphore_signal(
            barrier, inc=1, device_id=(((a_me + n // 16) % 4) * 4 + x, (g + n) % 16), device_id_type=MESH
        )
    for dev in (left, right):
        pl.semaphore_signal(barrier, inc=1, device_id=dev, device_id_type=MESH)

    lane16 = lax.broadcasted_iota(jnp.int32, (16, 128), 1) < HD

    def prepare(t):
        fetch[t].wait()

        def body(p, carry):
            both = raw[t, :, pl.ds(pl.multiple_of(p * 128, 128), 128)].astype(F32)
            turned = pltpu.roll(both, HD, 1)
            sendbuf[t * 48 + 2 * p] = jnp.where(lane16, both[0:16], turned[16:32]).astype(BF16)
            sendbuf[t * 48 + 2 * p + 1] = jnp.where(lane16, turned[0:16], both[16:32]).astype(BF16)
            return carry

        lax.fori_loop(0, 24, body, 0, unroll=4)

    for t in range(3):
        prepare(t)
    fetch[3].wait()
    fetch[4].wait()
    pl.semaphore_wait(barrier, 65)

    def send_wave(t, target):
        def body(n, carry):
            h = (n + 3 * g) % 48
            gd, kd = h // 3, h % 3
            ad = ((gd // 2) % 4 + 1 + kd) % 4
            here = (ad == a_me) & (gd == g)
            src = sendbuf.at[t * 48 + h]

            @pl.when(jnp.logical_not(here))
            def _():
                remote(src, target, e_send, e_recv.at[t, a_me], (ad * 4 + x, gd)).start()

            @pl.when(here)
            def _():
                pltpu.make_async_copy(src, target, e_recv.at[t, a_me]).start()

            return carry

        lax.fori_loop(0, 48, body, 0)

    send_wave(0, kbuf.at[0, a_me, g])
    send_wave(1, vbuf.at[0, a_me, g])
    send_wave(2, qbuf.at[a_me, g])

    def wcols(yy):
        return w_hbm.at[:, pl.ds(pl.multiple_of(yy * 768, 128), 768)]

    w1 = []
    for r in range(1, 4):
        yd = (y + r) % 4
        cp = remote(
            wcols(yd), wbuf.at[y, zh], w1_send.at[r - 1], w1_recv.at[r - 1], (seq, zh * 8 + yd * 2 + c)
        )
        cp.start()
        w1.append(cp)
    w1_own = pltpu.make_async_copy(wcols(y), wbuf.at[y, zh], w1_loc)
    w1_own.start()

    def x_copy(direction, t, a):
        buf = (kbuf, vbuf)[t]
        return remote(
            buf.at[0, a], buf.at[1 + direction, a],
            x_send.at[direction, t, a], x_recv.at[direction, t, a], (right, left)[direction],
        )

    def f_copy(t, a):
        buf = (kbuf, vbuf)[t]
        direction = a // 2
        return remote(
            buf.at[1 + direction, a], buf.at[3, a], f_send.at[t, a], f_recv.at[t, a], (right, left)[direction]
        )

    def pass_on(t, a):
        x_copy(a // 2, t, a).wait_recv()
        f_copy(t, a).start()

    half_lane = lax.broadcasted_iota(jnp.int32, (8, 128), 1) < HD

    def tile_rows(n, carry):
        midx, i = n // 4, n % 4
        for jt in range(2):
            one = jnp.where(mask[midx, i, 2 * jt] > 0, 0.0, NEG).astype(F32)
            two = jnp.where(mask[midx, i, 2 * jt + 1] > 0, 0.0, NEG).astype(F32)
            tiles[midx, i, jt] = jnp.where(half_lane, one, two)
        return carry

    @pl.when(active)
    def _():
        lax.fori_loop(0, 36, tile_rows, 0)
        tiles[9] = jnp.full((4, 2, 8, 128), NEG, F32)
        for t in range(2):
            buf = (kbuf, vbuf)[t]
            for a in (0, 2, 1, 3):
                arrived(buf.at[0, a], e_recv.at[t, a])
                x_copy(0, t, a).start()
                x_copy(1, t, a).start()
        for a in (0, 2, 1, 3):
            pass_on(0, a)
        lane = lax.broadcasted_iota(jnp.int32, (256, 128), 1) < HD
        for a in range(4):
            arrived(qbuf.at[a], e_recv.at[2, a])
            both = qbuf[a].astype(F32).reshape(256, 128)
            lo = jnp.where(lane, both, 0.0)
            hi = jnp.where(lane, 0.0, both)
            qlo[a, 0:256] = lo.astype(BF16)
            qlo[a, 256:512] = pltpu.roll(hi, HD, 1).astype(BF16)
            qhi[a, 0:256] = pltpu.roll(lo, HD, 1).astype(BF16)
            qhi[a, 256:512] = hi.astype(BF16)

    for cp in w1:
        cp.wait()
    w1_own.wait()
    w2 = remote(
        wbuf.at[x, zh], wbuf.at[x, zh], w2_send, w2_recv, ((3 - a_me) * 4 + x, other * 8 + y * 2 + c)
    )
    w2f = remote(
        wbuf.at[x, other], wbuf.at[x, other], w2f_send, w2_recv, ((1 + a_me // 3) * 4 + x, g)
    )
    w3r = remote(wbuf.at[x, other], wbuf.at[x, other], w3_send.at[0], w3_recv.at[0], right)
    w3l = remote(wbuf.at[x, other], wbuf.at[x, other], w3_send.at[1], w3_recv.at[1], left)

    @pl.when(boundary)
    def _():
        w2.start()

    lane512 = lax.broadcasted_iota(jnp.int32, (512, 128), 1) < HD

    def update(a, blocks, first):
        scores = []
        for buf, ap, _ in blocks:
            keys = kbuf[buf, ap].reshape(256, 128)
            for q in (qlo, qhi):
                scores.append(
                    lax.dot_general(q[a], keys, (((1,), (1,)), ((), ())), preferred_element_type=F32)
                )
        weights = [[] for _ in scores]
        alphas = []
        for n in range(8):
            rows = slice(n * 64, (n + 1) * 64)
            cols = []
            for b, (_, _, midx) in enumerate(blocks):
                for jt in range(2):
                    hide = tiles[midx, n % 4, jt][None]
                    for half in range(2):
                        tile = scores[2 * b + half][rows, jt * 128:(jt + 1) * 128]
                        cols.append(((b, half), (tile.reshape(8, 8, 128) + hide).reshape(64, 128)))
            top = jnp.max(functools.reduce(jnp.maximum, [tile for _, tile in cols]), axis=1, keepdims=True)
            if first:
                m_new = jnp.broadcast_to(top, (64, 128))
                total = None
            else:
                m_old = m_ref[a, rows]
                m_new = jnp.maximum(m_old, top)
                alpha = jnp.exp2((m_old - m_new) * SCALE2)
                alphas.append(alpha)
                total = l_ref[a, rows] * alpha
            m_ref[a, rows] = m_new
            found = {}
            for key, tile in cols:
                w = jnp.exp2((tile - m_new) * SCALE2)
                total = w if total is None else total + w
                found.setdefault(key, []).append(w.astype(BF16))
            l_ref[a, rows] = total
            for (b, half), ws in found.items():
                weights[2 * b + half].append(jnp.concatenate(ws, axis=1))
        sums = [None, None]
        for n, (ws, (buf, ap, _)) in enumerate(zip(weights, [blk for blk in blocks for _ in range(2)])):
            values = vbuf[buf, ap].reshape(256, 128)
            res = jnp.dot(jnp.concatenate(ws, axis=0), values, preferred_element_type=F32)
            sums[n % 2] = res if sums[n % 2] is None else sums[n % 2] + res
        new = jnp.where(lane512, sums[0], sums[1])
        if first:
            acc_ref[a] = new
        else:
            acc_ref[a] = acc_ref[a] * jnp.concatenate(alphas, axis=0) + new

    def local(a, carry):
        blocks = []
        for ap in range(4):
            off = ap - a
            midx = jnp.where(off > 0, 4 + 2 * off, 3 - 2 * off)
            midx = jnp.where(off == 0, 0, midx)
            blocks.append((0, ap, jnp.where((off > 2) | (off < -2), 9, midx)))
        update(a, blocks, True)
        return carry

    def pair(buf_minus, buf_plus, step_minus, step_plus, midx):
        def body(a):
            minus, plus = a - step_minus, a + step_plus
            update(
                a,
                [
                    (buf_minus, jnp.maximum(minus, 0), jnp.where(minus >= 0, midx, 9)),
                    (buf_plus, jnp.minimum(plus, 3), jnp.where(plus <= 3, midx + 1, 9)),
                ],
                False,
            )

        return body

    near = pair(1, 2, (3 - x) // 3, (x + 1) // 4, 1)
    far = pair(3, 3, (3 - x) // 2, (x + 2) // 4, 3)

    @pl.when(active)
    def _():
        lax.fori_loop(0, 2, local, 0)
        for a in (0, 2, 1, 3):
            pass_on(1, a)

    @pl.when(boundary)
    def _():
        w2.wait_recv()
        w2f.start()

    @pl.when(active)
    def _():
        lax.fori_loop(2, 4, local, 0)
        for t in range(2):
            for a in range(4):
                x_copy(1 - a // 2, t, a).wait_recv()

        def step(a, carry):
            near(a)
            return carry

        lax.fori_loop(0, 4, step, 0)

    @pl.when(jnp.logical_not(boundary))
    def _():
        w2.wait_recv()

    w3r.start()
    w3l.start()

    lane256 = lax.broadcasted_iota(jnp.int32, (256, 128), 1) < HD

    @pl.when(active)
    def _():
        for t in range(2):
            for a in range(4):
                f_copy(t, a).wait_recv()

        def step(a, carry):
            far(a)
            total = jnp.sum(l_ref[a], axis=1, keepdims=True)
            acc = acc_ref[a]
            att = (acc + pltpu.roll(acc, HD, 1)) / total
            packed = jnp.where(lane256, att[0:256], att[256:512]).astype(BF16)
            slot = zh * 3 + k_me
            for hd in range(2):
                opack[2 * a + hd] = packed[hd * 128:(hd + 1) * 128]
                here = (a_me == a) & (zh == hd)
                src, dst = opack.at[2 * a + hd], attended.at[0, slot]

                @pl.when(jnp.logical_not(here))
                def _():
                    remote(src, dst, o_send, o_recv.at[slot], (a * 4 + x, hd * 8 + y * 2 + c)).start()

                @pl.when(here)
                def _():
                    pltpu.make_async_copy(src, dst, o_recv.at[slot]).start()

            return carry

        lax.fori_loop(0, 4, step, 0)

    def a_copy(direction, slot):
        return remote(
            attended.at[0, slot], attended.at[1 + direction, slot],
            a_send.at[direction, slot], a_recv.at[direction, slot], (ynext, yprev)[direction],
        )

    def af_copy(slot):
        direction = slot // 3
        return remote(
            attended.at[1 + direction, slot], attended.at[3, slot],
            af_send.at[slot], af_recv.at[slot], (ynext, yprev)[direction],
        )

    for slot in SLOTS:
        arrived(attended.at[0, slot], o_recv.at[slot])
        a_copy(0, slot).start()
        a_copy(1, slot).start()

    xl, xr = (x + 3) % 4, (x + 1) % 4
    w3r.wait_recv()
    src_l = wbuf.at[xl, other, pl.ds(0, 96)]
    w3fr = remote(src_l, src_l, w3f_send.at[0], w3f_recv.at[0], right)
    w3fr.start()
    w3l.wait_recv()
    src_r = wbuf.at[xr, other, pl.ds(96, 96)]
    w3fl = remote(src_r, src_r, w3f_send.at[1], w3f_recv.at[1], left)
    w3fl.start()

    for slot in SLOTS:
        a_copy(slot // 3, slot).wait_recv()
        af_copy(slot).start()

    lane128 = lax.broadcasted_iota(jnp.int32, (128, 128), 1) < HD

    def unpack(r):
        for t in range(3):
            x0 = attended[r, 2 * t].astype(F32)
            x1 = attended[r, 2 * t + 1].astype(F32)
            cols = slice(r * 384 + t * 128, r * 384 + (t + 1) * 128)
            lo = jnp.where(lane128, x0, pltpu.roll(x1, HD, 1)).astype(BF16).reshape(4, 2, 16, 128)
            hi = jnp.where(lane128, pltpu.roll(x0, HD, 1), x1).astype(BF16).reshape(4, 2, 16, 128)
            for cd in range(2):
                lhs[cd, :, 0, :, cols] = lo[:, cd]
                lhs[cd, :, 1, :, cols] = hi[:, cd]

    unpack(0)
    for slot in SLOTS:
        a_copy(1 - slot // 3, slot).wait_recv()
    unpack(1)
    unpack(2)
    w3fr.wait_recv()
    w3fl.wait_recv()
    for slot in SLOTS:
        af_copy(slot).wait_recv()
    unpack(3)

    owners = (y, (y + 3) % 4, (y + 1) % 4, (y + 2) % 4)

    def project(core, n):
        rows = lhs[core].reshape(128, 1536)
        res = None
        for r in range(4):
            rhs = wbuf[owners[r], :, :, n * 256:(n + 1) * 256].reshape(384, 256)
            d = jnp.dot(rows[:, r * 384:(r + 1) * 384], rhs, preferred_element_type=F32)
            res = d if res is None else res + d
        return res

    def d_copy(n):
        return remote(part.at[n], dpart.at[n], d_send.at[n], d_recv.at[n], (seq, g + 1 - 2 * c))

    def y_copy(n, r):
        yd = (y + r) % 4
        cols = pl.ds(pl.multiple_of(y * 768 + n * 256, 128), 256)
        return remote(
            fin.at[n, yd], o_ref.at[:, cols], y_send.at[n, r - 1], y_recv.at[n, r - 1],
            (seq, zh * 8 + yd * 2 + c),
        )

    for n in range(3):
        part[n] = project(1 - c, n)
        d_copy(n).start()
    for n in range(3):
        mine = project(c, n)
        cols = pl.ds(pl.multiple_of(y * 768 + n * 256, 128), 256)
        d_copy(n).wait_recv()
        done = (mine + dpart[n] + bias_ref[cols].astype(F32)[None]).astype(BF16)
        fin[n] = done.reshape(4, 32, 256)
        for r in range(1, 4):
            y_copy(n, r).start()
        o_ref[:, cols] = fin[n, y]

    @pl.when(active)
    def _():
        arrived(sendbuf.at[pl.ds(0, 141)], e_send)
        for t in range(2):
            for a in range(4):
                x_copy(0, t, a).wait_send()
                x_copy(1, t, a).wait_send()
                f_copy(t, a).wait_send()
        arrived(opack.at[pl.ds(0, 7)], o_send)

    @pl.when(jnp.logical_not(active))
    def _():
        arrived(sendbuf, e_send)

    @pl.when(boundary)
    def _():
        w2.wait_send()
        w2f.wait_send()

    for cp in (w3r, w3l, w3fr, w3fl):
        cp.wait_send()
    for slot in range(6):
        a_copy(0, slot).wait_send()
        a_copy(1, slot).wait_send()
        af_copy(slot).wait_send()
    for n in range(3):
        d_copy(n).wait_send()
        for r in range(1, 4):
            y_copy(n, r).wait()


def shards(query_in, key_in, value_in, block_mask, out_weight, out_bias):
    hbm = pl.BlockSpec(memory_space=pltpu.HBM)
    dma = pltpu.SemaphoreType.DMA
    return pl.pallas_call(
        kernel,
        out_shape=jax.ShapeDtypeStruct((32, 3072), BF16),
        in_specs=[hbm] * 6,
        out_specs=pl.BlockSpec(memory_space=pltpu.VMEM),
        scratch_shapes=[
            pltpu.VMEM((3, 32, 3072), BF16),
            pltpu.SMEM((9, 4, 4), jnp.int32),
            pltpu.VMEM((3072,), BF16),
            pltpu.VMEM((144, 16, 128), BF16),
            pltpu.VMEM((4, 4, 16, 16, 128), BF16),
            pltpu.VMEM((4, 4, 16, 16, 128), BF16),
            pltpu.VMEM((4, 16, 16, 128), BF16),
            pltpu.VMEM((4, 512, 128), BF16),
            pltpu.VMEM((4, 512, 128), BF16),
            pltpu.VMEM((10, 4, 2, 8, 128), F32),
            pltpu.VMEM((4, 512, 128), F32),
            pltpu.VMEM((4, 512, 128), F32),
            pltpu.VMEM((4, 512, 128), F32),
            pltpu.VMEM((8, 128, 128), BF16),
            pltpu.VMEM((4, 6, 128, 128), BF16),
            pltpu.VMEM((2, 4, 2, 16, 1536), BF16),
            pltpu.VMEM((4, 2, 192, 768), BF16),
            pltpu.VMEM((3, 128, 256), F32),
            pltpu.VMEM((3, 128, 256), F32),
            pltpu.VMEM((3, 4, 32, 256), BF16),
            dma((5,)), dma, dma((3, 4)), dma((2, 2, 4)), dma((2, 2, 4)), dma((2, 4)), dma((2, 4)),
            dma((3,)), dma((3,)), dma, dma, dma, dma, dma((2,)), dma((2,)), dma((2,)), dma((2,)),
            dma, dma((6,)), dma((2, 6)), dma((2, 6)), dma((6,)), dma((6,)),
            dma((3,)), dma((3,)), dma((3, 3)), dma((3, 3)),
        ],
        compiler_params=pltpu.CompilerParams(
            collective_id=0, has_side_effects=True, vmem_limit_bytes=63 * 1024 * 1024
        ),
        name="radial",
    )(query_in, key_in, value_in, block_mask, out_weight, out_bias)


def solution(mesh):
    return jax.shard_map(
        shards,
        mesh=mesh,
        in_specs=(
            P(("seq", "head"), None),
            P(("seq", "head"), None),
            P(("seq", "head"), None),
            P(),
            P("head", None),
            P(),
        ),
        out_specs=P(("seq", "head"), None),
        check_vma=False,
    )
```

time: 336 us -> 80.1 us (0.24)
  waiting for transfers between devices: 143 us -> 0 us
  starting transfers between devices: 78 us -> 0 us
  Pallas kernels: 0 us -> 75.7 us
  matrix products: 56.6 us -> 0 us
  local copies, waits for them, and re-layouts: 27.3 us -> 3.02 us
  other arithmetic: 15.4 us -> 0 us
  between operations: 13.9 us -> 0.01 us
    reduce_scatter x1 -> x0, waiting for transfers between devices: 127 us -> none  [shards(): lax.psum_scatter(jnp.dot(attended, out_weight, preferred_element_type=jnp...]
    pallas_call x0 -> x1, Pallas kernels: none -> 75.7 us  [shards(): pl.pallas_call(kernel, out_shape=jax.ShapeDtypeStruct((32, 3072), BF16),...]
    dot_general x19 -> x0, matrix products: 56.6 us -> none  [the longest x9 30.7 us: shards(): jnp.einsum('hqk,khd->qhd', weights.astype(jnp.bfloat16), values_here, pre...]
    ppermute x16 -> x0, starting transfers between devices: 56.1 us -> none  [shifted(): lax.ppermute(value, axis, [(source, source + steps) for source in range(f...]
    all_to_all x3 -> x0, starting transfers between devices: 22 us -> none  [the longest x1 12.6 us: shards(): lax.all_to_all(query_in, 'head', split_axis=1, concat_axis=0, tiled=True)]
    all_to_all x3 -> x0, waiting for transfers between devices: 16.5 us -> none  [the longest x1 9.74 us: shards(): lax.all_to_all(key_in, 'head', split_axis=1, concat_axis=0, tiled=True)]
    ppermute x16 -> x0, local copies, waits for them, and re-layouts: 14.7 us -> none  [shifted(): lax.ppermute(value, axis, [(source, source + steps) for source in range(f...]
    reduce_sum x1 -> x0, other arithmetic: 12.5 us -> none  [shards(): total = total + jnp.sum(weights, axis=2)]
  transfers between devices with their start and end apart: 20 -> 0, of which waited for: 3 -> 0; matrix products, arithmetic and copies ran while one was open for 25% -> 0% of each run, Pallas kernels for 0% -> 0%
where the time goes in v2:
time: 80.1 us; the launch traced here: 78.7 us
  Pallas kernels  75.7 us (95%)
  local copies, waits for them, and re-layouts  3.02 us (4%)
    pallas_call x1, Pallas kernels, shards(): pl.pallas_call(kernel, out_shape=jax.ShapeDtypeStruct((32, 3072), BF16),...  75.7 us
    unnamed x2, local copies, waits for them, and re-layouts  3.02 us

profile of v2, /device:TPU:1, one launch (start us, length us, event | category | flops | bytes accessed | tf_op | source)
XLA Modules:
  0.0 78.7 jit_solution(11281951776777888169)
XLA Ops:
  0.0 1.4 %copy.7.mask_hbm = s32[9,4,4]{2,1,0:T(4,128)} copy(s32[9,4,4]{0,2,1:T(4,128)} %param.9) | data formatting | bytes 1152 | tf_op args[3]
  1.4 75.7 %radial.1 = bf16[32,3072]{1,0:T(8,128)(2,1)} custom-call(bf16[32,3072]{1,0:T(8,128)(2,1)} %q_hbm.1, bf16[32,3072]{1,0:T(8,128)(2,1)} %k_hbm.1, bf16[32,3072]{1,0:T(8,128)(2,1)} %v_hbm.1, s32[9,4,4]{2,1,0:T(4,128)} %copy.7.mask_hbm, bf16[192,3072]{1,0:T(8,128)(2,1)} %w_hbm.1, bf16[3072]{0:T(1024)(128)(2,1)} %bias_hbm.1), custom_call_target="tpu_custom_call" | custom-call | tf_op jit(solution)/shard_map/radial/pallas_call | solution.py:455
  77.1 1.6 %copy.9 = bf16[32,3072]{1,0:T(8,128)(2,1)} copy(bf16[32,3072]{1,0:T(8,128)(2,1)} %radial.1) | data formatting | bytes 393216

commit v3 on v2

--- a/solution.py
+++ b/solution.py
@@ -101,23 +101,23 @@
 
         lax.fori_loop(0, 48, body, 0)
 
+    def w1_copy(dx, r):
+        yd, xx = (y + r) % 4, (x + dx) % 4
+        rows = pl.ds(pl.multiple_of(xx * 48, 16), 48)
+        return remote(
+            w_hbm.at[rows, pl.ds(pl.multiple_of(yd * 768, 128), 768)], wbuf.at[y, zh, rows],
+            w1_send.at[dx, r - 1], w1_recv.at[dx, r - 1], (seq, zh * 8 + yd * 2 + c),
+        )
+
+    w1_own = pltpu.make_async_copy(
+        w_hbm.at[:, pl.ds(pl.multiple_of(y * 768, 128), 768)], wbuf.at[y, zh], w1_loc
+    )
+    w1_own.start()
     send_wave(0, kbuf.at[0, a_me, g])
+    for r in range(1, 4):
+        w1_copy(0, r).start()
     send_wave(1, vbuf.at[0, a_me, g])
     send_wave(2, qbuf.at[a_me, g])
-
-    def wcols(yy):
-        return w_hbm.at[:, pl.ds(pl.multiple_of(yy * 768, 128), 768)]
-
-    w1 = []
-    for r in range(1, 4):
-        yd = (y + r) % 4
-        cp = remote(
-            wcols(yd), wbuf.at[y, zh], w1_send.at[r - 1], w1_recv.at[r - 1], (seq, zh * 8 + yd * 2 + c)
-        )
-        cp.start()
-        w1.append(cp)
-    w1_own = pltpu.make_async_copy(wcols(y), wbuf.at[y, zh], w1_loc)
-    w1_own.start()
 
     def x_copy(direction, t, a):
         buf = (kbuf, vbuf)[t]
@@ -142,8 +142,8 @@
     def tile_rows(n, carry):
         midx, i = n // 4, n % 4
         for jt in range(2):
-            one = jnp.where(mask[midx, i, 2 * jt] > 0, 0.0, NEG).astype(F32)
-            two = jnp.where(mask[midx, i, 2 * jt + 1] > 0, 0.0, NEG).astype(F32)
+            one = jnp.where(mask[i, 2 * jt, midx] > 0, 0.0, NEG).astype(F32)
+            two = jnp.where(mask[i, 2 * jt + 1, midx] > 0, 0.0, NEG).astype(F32)
             tiles[midx, i, jt] = jnp.where(half_lane, one, two)
         return carry
 
@@ -157,6 +157,48 @@
                 arrived(buf.at[0, a], e_recv.at[t, a])
                 x_copy(0, t, a).start()
                 x_copy(1, t, a).start()
+
+    my_rows = pl.ds(pl.multiple_of(x * 48, 16), 48)
+
+    def w2_copy(n):
+        ref = wbuf.at[pl.ds(2 * n, 2), zh, my_rows]
+        dev = ((3 - a_me) * 4 + x, other * 8 + y * 2 + c)
+        return remote(ref, ref, w2_send.at[n], w2_recv.at[n], dev)
+
+    def w2f_copy(n):
+        ref = wbuf.at[pl.ds(2 * n, 2), other, my_rows]
+        return remote(ref, ref, w2f_send.at[n], w2_recv.at[n], ((1 + a_me // 3) * 4 + x, g))
+
+    def w3_copy(direction):
+        ref = wbuf.at[:, other, my_rows]
+        return remote(ref, ref, w3_send.at[direction], w3_recv.at[direction], (right, left)[direction])
+
+    def w3f_copy(direction):
+        xx = (x + (3, 1)[direction]) % 4
+        ref = wbuf.at[pl.ds(2 * direction, 2), other, pl.ds(pl.multiple_of(xx * 48, 16), 48)]
+        return remote(ref, ref, w3f_send.at[direction], w3f_recv.at[direction], (right, left)[direction])
+
+    def w2_forward(n):
+        @pl.when(boundary)
+        def _():
+            w2_copy(n).wait_recv()
+            w2f_copy(n).start()
+
+    @pl.when(jnp.logical_not(active))
+    def _():
+        arrived(sendbuf, e_send)
+
+    for r in range(1, 4):
+        w1_copy(0, r).wait()
+    w1_own.wait()
+
+    @pl.when(boundary)
+    def _():
+        w2_copy(0).start()
+        w2_copy(1).start()
+
+    @pl.when(active)
+    def _():
         for a in (0, 2, 1, 3):
             pass_on(0, a)
         lane = lax.broadcasted_iota(jnp.int32, (256, 128), 1) < HD
@@ -170,21 +212,9 @@
             qhi[a, 0:256] = pltpu.roll(lo, HD, 1).astype(BF16)
             qhi[a, 256:512] = hi.astype(BF16)
 
-    for cp in w1:
-        cp.wait()
-    w1_own.wait()
-    w2 = remote(
-        wbuf.at[x, zh], wbuf.at[x, zh], w2_send, w2_recv, ((3 - a_me) * 4 + x, other * 8 + y * 2 + c)
-    )
-    w2f = remote(
-        wbuf.at[x, other], wbuf.at[x, other], w2f_send, w2_recv, ((1 + a_me // 3) * 4 + x, g)
-    )
-    w3r = remote(wbuf.at[x, other], wbuf.at[x, other], w3_send.at[0], w3_recv.at[0], right)
-    w3l = remote(wbuf.at[x, other], wbuf.at[x, other], w3_send.at[1], w3_recv.at[1], left)
-
-    @pl.when(boundary)
-    def _():
-        w2.start()
+    for dx in range(1, 4):
+        for r in range(1, 4):
+            w1_copy(dx, r).start()
 
     lane512 = lax.broadcasted_iota(jnp.int32, (512, 128), 1) < HD
 
@@ -264,51 +294,56 @@
     near = pair(1, 2, (3 - x) // 3, (x + 1) // 4, 1)
     far = pair(3, 3, (3 - x) // 2, (x + 2) // 4, 3)
 
-    @pl.when(active)
-    def _():
-        lax.fori_loop(0, 2, local, 0)
+    def near_step(a, carry):
+        near(a)
+        return carry
+
+    @pl.when(active)
+    def _():
+        lax.fori_loop(0, 1, local, 0)
+
+    w2_forward(0)
+
+    @pl.when(active)
+    def _():
+        lax.fori_loop(1, 2, local, 0)
         for a in (0, 2, 1, 3):
             pass_on(1, a)
-
-    @pl.when(boundary)
-    def _():
-        w2.wait_recv()
-        w2f.start()
-
-    @pl.when(active)
-    def _():
-        lax.fori_loop(2, 4, local, 0)
+        lax.fori_loop(2, 3, local, 0)
+
+    w2_forward(1)
+
+    @pl.when(active)
+    def _():
+        lax.fori_loop(3, 4, local, 0)
         for t in range(2):
             for a in range(4):
                 x_copy(1 - a // 2, t, a).wait_recv()
-
-        def step(a, carry):
-            near(a)
-            return carry
-
-        lax.fori_loop(0, 4, step, 0)
-
-    @pl.when(jnp.logical_not(boundary))
-    def _():
-        w2.wait_recv()
-
-    w3r.start()
-    w3l.start()
-
-    lane256 = lax.broadcasted_iota(jnp.int32, (256, 128), 1) < HD
-
-    @pl.when(active)
-    def _():
+        lax.fori_loop(0, 4, near_step, 0)
         for t in range(2):
             for a in range(4):
                 f_copy(t, a).wait_recv()
 
-        def step(a, carry):
+    @pl.when(jnp.logical_not(boundary))
+    def _():
+        w2_copy(0).wait_recv()
+        w2_copy(1).wait_recv()
+
+    w3_copy(0).start()
+    w3_copy(1).start()
+
+    lane256 = lax.broadcasted_iota(jnp.int32, (256, 128), 1) < HD
+
+    @pl.when(active)
+    def _():
+        def step(n, carry):
+            a = (a_me + n) % 4
             far(a)
-            total = jnp.sum(l_ref[a], axis=1, keepdims=True)
+            total = jnp.broadcast_to(jnp.sum(l_ref[a], axis=1, keepdims=True), (512, 128))
             acc = acc_ref[a]
-            att = (acc + pltpu.roll(acc, HD, 1)) / total
-            packed = jnp.where(lane256, att[0:256], att[256:512]).astype(BF16)
+            att = acc + pltpu.roll(acc, HD, 1)
+            packed = jnp.where(lane256, att[0:256], att[256:512])
+            packed = (packed / jnp.where(lane256, total[0:256], total[256:512])).astype(BF16)
             slot = zh * 3 + k_me
             for hd in range(2):
                 opack[2 * a + hd] = packed[hd * 128:(hd + 1) * 128]
@@ -333,31 +368,50 @@
             a_send.at[direction, slot], a_recv.at[direction, slot], (ynext, yprev)[direction],
         )
 
-    def af_copy(slot):
-        direction = slot // 3
+    def af_copy(direction, slot):
         return remote(
             attended.at[1 + direction, slot], attended.at[3, slot],
             af_send.at[slot], af_recv.at[slot], (ynext, yprev)[direction],
         )
 
-    for slot in SLOTS:
-        arrived(attended.at[0, slot], o_recv.at[slot])
-        a_copy(0, slot).start()
-        a_copy(1, slot).start()
-
-    xl, xr = (x + 3) % 4, (x + 1) % 4
-    w3r.wait_recv()
-    src_l = wbuf.at[xl, other, pl.ds(0, 96)]
-    w3fr = remote(src_l, src_l, w3f_send.at[0], w3f_recv.at[0], right)
-    w3fr.start()
-    w3l.wait_recv()
-    src_r = wbuf.at[xr, other, pl.ds(96, 96)]
-    w3fl = remote(src_r, src_r, w3f_send.at[1], w3f_recv.at[1], left)
-    w3fl.start()
-
-    for slot in SLOTS:
-        a_copy(slot // 3, slot).wait_recv()
-        af_copy(slot).start()
+    def slot_of(n, yy, zz, act):
+        k = (a_me + 15 - n - yy) % 4
+
+        @pl.when(k < 3)
+        def _():
+            act(zz * 3 + k)
+
+    def gather(n):
+        for zz in range(2):
+
+            def act(slot):
+                arrived(attended.at[0, slot], o_recv.at[slot])
+                a_copy(0, slot).start()
+                a_copy(1, slot).start()
+
+            slot_of(n, y, zz, act)
+
+    def a_forward(n):
+        for direction in range(2):
+
+            def act(slot):
+                a_copy(direction, slot).wait_recv()
+                af_copy(direction, slot).start()
+
+            slot_of(n, y + (3, 1)[direction], direction, act)
+
+    gather(0)
+    gather(1)
+    a_forward(0)
+    gather(2)
+    a_forward(1)
+    gather(3)
+    a_forward(2)
+    a_forward(3)
+
+    for direction in range(2):
+        w3_copy(direction).wait_recv()
+        w3f_copy(direction).start()
 
     lane128 = lax.broadcasted_iota(jnp.int32, (128, 128), 1) < HD
 
@@ -377,11 +431,15 @@
         a_copy(1 - slot // 3, slot).wait_recv()
     unpack(1)
     unpack(2)
-    w3fr.wait_recv()
-    w3fl.wait_recv()
     for slot in SLOTS:
-        af_copy(slot).wait_recv()
+        af_copy(slot // 3, slot).wait_recv()
     unpack(3)
+
+    for direction in range(2):
+        w3f_copy(direction).wait_recv()
+    for dx in range(1, 4):
+        for r in range(1, 4):
+            w1_copy(dx, r).wait()
 
     owners = (y, (y + 3) % 4, (y + 1) % 4, (y + 2) % 4)
 
@@ -428,21 +486,19 @@
                 f_copy(t, a).wait_send()
         arrived(opack.at[pl.ds(0, 7)], o_send)
 
-    @pl.when(jnp.logical_not(active))
-    def _():
-        arrived(sendbuf, e_send)
-
     @pl.when(boundary)
     def _():
-        w2.wait_send()
-        w2f.wait_send()
-
-    for cp in (w3r, w3l, w3fr, w3fl):
-        cp.wait_send()
+        for n in range(2):
+            w2_copy(n).wait_send()
+            w2f_copy(n).wait_send()
+
+    for direction in range(2):
+        w3_copy(direction).wait_send()
+        w3f_copy(direction).wait_send()
     for slot in range(6):
         a_copy(0, slot).wait_send()
         a_copy(1, slot).wait_send()
-        af_copy(slot).wait_send()
+        af_copy(slot // 3, slot).wait_send()
     for n in range(3):
         d_copy(n).wait_send()
         for r in range(1, 4):
@@ -459,7 +515,7 @@
         out_specs=pl.BlockSpec(memory_space=pltpu.VMEM),
         scratch_shapes=[
             pltpu.VMEM((3, 32, 3072), BF16),
-            pltpu.SMEM((9, 4, 4), jnp.int32),
+            pltpu.SMEM((4, 4, 9), jnp.int32),
             pltpu.VMEM((3072,), BF16),
             pltpu.VMEM((144, 16, 128), BF16),
             pltpu.VMEM((4, 4, 16, 16, 128), BF16),
@@ -479,7 +535,7 @@
             pltpu.VMEM((3, 128, 256), F32),
             pltpu.VMEM((3, 4, 32, 256), BF16),
             dma((5,)), dma, dma((3, 4)), dma((2, 2, 4)), dma((2, 2, 4)), dma((2, 4)), dma((2, 4)),
-            dma((3,)), dma((3,)), dma, dma, dma, dma, dma((2,)), dma((2,)), dma((2,)), dma((2,)),
+            dma((4, 3)), dma((4, 3)), dma, dma((2,)), dma((2,)), dma((2,)), dma((2,)), dma((2,)), dma((2,)), dma((2,)),
             dma, dma((6,)), dma((2, 6)), dma((2, 6)), dma((6,)), dma((6,)),
             dma((3,)), dma((3,)), dma((3, 3)), dma((3, 3)),
         ],
@@ -487,7 +543,7 @@
             collective_id=0, has_side_effects=True, vmem_limit_bytes=63 * 1024 * 1024
         ),
         name="radial",
-    )(query_in, key_in, value_in, block_mask, out_weight, out_bias)
+    )(query_in, key_in, value_in, jnp.transpose(block_mask, (1, 2, 0)), out_weight, out_bias)
 
 
 def solution(mesh):

time: 80.1 us -> 70.5 us (0.88); the launches traced: 78.7 us -> 70.4 us
  Pallas kernels: 75.7 us -> 68.8 us
  local copies, waits for them, and re-layouts: 3.02 us -> 1.62 us
    pallas_call x1, Pallas kernels: 75.7 us -> 68.8 us  [shards(): pl.pallas_call(kernel, out_shape=jax.ShapeDtypeStruct((32, 3072), BF16),...]
    unnamed x2 -> x1, local copies, waits for them, and re-layouts: 3.02 us -> 1.62 us
where the time goes in v3:
time: 70.5 us; the launch traced here: 70.4 us
  Pallas kernels  68.8 us (98%)
  local copies, waits for them, and re-layouts  1.62 us (2%)
    pallas_call x1, Pallas kernels, shards(): pl.pallas_call(kernel, out_shape=jax.ShapeDtypeStruct((32, 3072), BF16),...  68.8 us
    unnamed x1, local copies, waits for them, and re-layouts  1.62 us

profile of v3, /device:TPU:1, one launch (start us, length us, event | category | flops | bytes accessed | tf_op | source)
XLA Modules:
  0.0 70.4 jit_solution(11404501743183832938)
XLA Ops:
  0.0 68.8 %radial.1 = bf16[32,3072]{1,0:T(8,128)(2,1)} custom-call(bf16[32,3072]{1,0:T(8,128)(2,1)} %q_hbm.1, bf16[32,3072]{1,0:T(8,128)(2,1)} %k_hbm.1, bf16[32,3072]{1,0:T(8,128)(2,1)} %v_hbm.1, s32[4,4,9]{2,1,0:T(4,128)} %bitcast.1, bf16[192,3072]{1,0:T(8,128)(2,1)} %w_hbm.1, bf16[3072]{0:T(1024)(128)(2,1)} %bias_hbm.1), custom_call_target="tpu_custom_call" | custom-call | tf_op jit(solution)/shard_map/radial/pallas_call | solution.py:511
  68.8 1.6 %copy.8 = bf16[32,3072]{1,0:T(8,128)(2,1)} copy(bf16[32,3072]{1,0:T(8,128)(2,1)} %radial.1) | data formatting | bytes 393216

commit v4 on v3

v4 whole, which is shorter than its diff:
```python
import functools
import math

import jax
import jax.numpy as jnp
from jax import lax
from jax.experimental import pallas as pl
from jax.experimental.pallas import tpu as pltpu
from jax.sharding import PartitionSpec as P

MESH = pl.DeviceIdType.MESH
F32 = jnp.float32
BF16 = jnp.bfloat16
HD = 64
NEG = -1e30
SCALE2 = math.log2(math.e) / math.sqrt(HD)


def kernel(
    q_hbm, k_hbm, v_hbm, mask_hbm, w_hbm, bias_hbm, o_ref,
    raw, mask, bias_ref, sendbuf, kbuf, vbuf, qbuf, qlo, qhi, tiles, sides, m_ref, acc_ref, opack,
    attended, lhs, wbuf, part, mine, dpart, fin,
    in_sem, e_send, e_recv, x_send, x_recv, fk_send, fk_recv, fv_send, fv_recv,
    w1_send, w1_recv, w1_loc, w2_send, w2_recv, w2f_send, w3_send, w3_recv, w3f_send, w3f_recv,
    o_send, o_recv, a_send, a_recv, d_send, d_recv, y_send, y_recv,
):
    seq = lax.axis_index("seq")
    g = lax.axis_index("head")
    a_me, x = seq // 4, seq % 4
    zh, y, c = g // 8, (g // 2) % 4, g % 2
    k_me = (a_me + 3 - y) % 4
    active = k_me < 3
    boundary = (a_me % 3) == 0
    right = (a_me * 4 + (x + 1) % 4, g)
    left = (a_me * 4 + (x + 3) % 4, g)
    other = 1 - zh

    def remote(src, dst, send, rcv, dev):
        return pltpu.make_async_remote_copy(
            src_ref=src, dst_ref=dst, send_sem=send, recv_sem=rcv, device_id=dev, device_id_type=MESH
        )

    def arrived(dst, sem):
        pltpu.make_async_copy(dst, dst, sem).wait()

    fetch = [
        pltpu.make_async_copy(src, raw.at[n], in_sem.at[n]) for n, src in enumerate((k_hbm, v_hbm, q_hbm))
    ]
    fetch.append(pltpu.make_async_copy(bias_hbm, bias_ref, in_sem.at[3]))
    fetch.append(pltpu.make_async_copy(mask_hbm, mask, in_sem.at[4]))
    for cp in fetch:
        cp.start()
    barrier = pltpu.get_barrier_semaphore()
    for n in range(1, 64):
        pl.semaphore_signal(
            barrier, inc=1, device_id=(((a_me + n // 16) % 4) * 4 + x, (g + n) % 16), device_id_type=MESH
        )
    for dev in (left, right):
        pl.semaphore_signal(barrier, inc=1, device_id=dev, device_id_type=MESH)

    lane16 = lax.broadcasted_iota(jnp.int32, (16, 128), 1) < HD

    def prepare(t):
        fetch[t].wait()

        def body(p, carry):
            both = raw[t, :, pl.ds(pl.multiple_of(p * 128, 128), 128)].astype(F32)
            turned = pltpu.roll(both, HD, 1)
            sendbuf[t * 48 + 2 * p] = jnp.where(lane16, both[0:16], turned[16:32]).astype(BF16)
            sendbuf[t * 48 + 2 * p + 1] = jnp.where(lane16, turned[0:16], both[16:32]).astype(BF16)
            return carry

        lax.fori_loop(0, 24, body, 0, unroll=4)

    for t in range(3):
        prepare(t)
    fetch[3].wait()
    fetch[4].wait()
    pl.semaphore_wait(barrier, 65)

    def send_wave(t, target):
        def body(n, carry):
            h = (n + 3 * g) % 48
            gd, kd = h // 3, h % 3
            ad = ((gd // 2) % 4 + 1 + kd) % 4
            here = (ad == a_me) & (gd == g)
            src = sendbuf.at[t * 48 + h]

            @pl.when(jnp.logical_not(here))
            def _():
                remote(src, target, e_send, e_recv.at[t, a_me], (ad * 4 + x, gd)).start()

            @pl.when(here)
            def _():
                pltpu.make_async_copy(src, target, e_recv.at[t, a_me]).start()

            return carry

        lax.fori_loop(0, 48, body, 0)

    def w1_copy(dx, r):
        yd, xx = (y + r) % 4, (x + dx) % 4
        rows = pl.ds(pl.multiple_of(xx * 48, 16), 48)
        return remote(
            w_hbm.at[rows, pl.ds(pl.multiple_of(yd * 768, 128), 768)], wbuf.at[y, zh, rows],
            w1_send.at[dx, r - 1], w1_recv.at[dx, r - 1], (seq, zh * 8 + yd * 2 + c),
        )

    w1_own = pltpu.make_async_copy(
        w_hbm.at[:, pl.ds(pl.multiple_of(y * 768, 128), 768)], wbuf.at[y, zh], w1_loc
    )
    w1_own.start()
    send_wave(0, kbuf.at[0, a_me, g])
    for r in range(1, 4):
        w1_copy(0, r).start()
    send_wave(1, vbuf.at[0, a_me, g])
    send_wave(2, qbuf.at[a_me, g])

    def x_copy(direction, t, a):
        buf = (kbuf, vbuf)[t]
        return remote(
            buf.at[0, a], buf.at[1 + direction, a],
            x_send.at[direction, t, a], x_recv.at[direction, t, a], (right, left)[direction],
        )

    def fk_copy(a):
        direction = a // 2
        return remote(
            kbuf.at[1 + direction, a], kbuf.at[3, a], fk_send.at[a], fk_recv.at[a], (right, left)[direction]
        )

    def fv_copy(direction, a):
        rows = pl.ds(8 * direction, 8)
        return remote(
            vbuf.at[1 + direction, a, rows], vbuf.at[3, a, rows],
            fv_send.at[direction, a], fv_recv.at[direction, a], (right, left)[direction],
        )

    def send_values(a):
        x_copy(0, 1, a).start()
        x_copy(1, 1, a).start()

    def pass_values(a):
        for direction in range(2):
            x_copy(direction, 1, a).wait_recv()
            fv_copy(direction, a).start()

    def got_values(a):
        fv_copy(0, a).wait_recv()
        fv_copy(1, a).wait_recv()

    half_lane = lax.broadcasted_iota(jnp.int32, (8, 128), 1) < HD

    def tile_rows(n, carry):
        midx, i = n // 4, n % 4
        for jt in range(2):
            one = jnp.where(mask[i, 2 * jt, midx] > 0, 0.0, NEG).astype(F32)
            two = jnp.where(mask[i, 2 * jt + 1, midx] > 0, 0.0, NEG).astype(F32)
            tiles[midx, i, jt] = jnp.where(half_lane, one, two)
        return carry

    @pl.when(active)
    def _():
        lax.fori_loop(0, 36, tile_rows, 0)
        tiles[9] = jnp.full((4, 2, 8, 128), NEG, F32)
        for a in (0, 2, 1, 3):
            arrived(kbuf.at[0, a], e_recv.at[0, a])
            x_copy(0, 0, a).start()
            x_copy(1, 0, a).start()
        for a in range(4):
            arrived(vbuf.at[0, a], e_recv.at[1, a])
            send_values(a)

    lane256 = lax.broadcasted_iota(jnp.int32, (256, 128), 1) < HD

    def value_sides(buf, ap):
        both = vbuf[buf, ap].astype(F32).reshape(256, 128)
        turned = pltpu.roll(both, HD, 1)
        lo = [jnp.where(lane256, v, 1.0).astype(BF16) for v in (both, turned)]
        hi = [jnp.where(lane256, 1.0, v).astype(BF16) for v in (turned, both)]
        return jnp.concatenate(lo, axis=0), jnp.concatenate(hi, axis=0)

    my_rows = pl.ds(pl.multiple_of(x * 48, 16), 48)

    def w2_copy(n):
        ref = wbuf.at[pl.ds(2 * n, 2), zh, my_rows]
        dev = ((3 - a_me) * 4 + x, other * 8 + y * 2 + c)
        return remote(ref, ref, w2_send.at[n], w2_recv.at[n], dev)

    def w2f_copy(n):
        ref = wbuf.at[pl.ds(2 * n, 2), other, my_rows]
        return remote(ref, ref, w2f_send.at[n], w2_recv.at[n], ((1 + a_me // 3) * 4 + x, g))

    def w3_copy(direction):
        ref = wbuf.at[:, other, my_rows]
        return remote(ref, ref, w3_send.at[direction], w3_recv.at[direction], (right, left)[direction])

    def w3f_copy(direction):
        xx = (x + (3, 1)[direction]) % 4
        ref = wbuf.at[pl.ds(2 * direction, 2), other, pl.ds(pl.multiple_of(xx * 48, 16), 48)]
        return remote(ref, ref, w3f_send.at[direction], w3f_recv.at[direction], (right, left)[direction])

    def w2_forward(n):
        @pl.when(boundary)
        def _():
            w2_copy(n).wait_recv()
            w2f_copy(n).start()

    @pl.when(jnp.logical_not(active))
    def _():
        arrived(sendbuf, e_send)

    for r in range(1, 4):
        w1_copy(0, r).wait()
    w1_own.wait()

    @pl.when(boundary)
    def _():
        w2_copy(0).start()
        w2_copy(1).start()

    @pl.when(active)
    def _():
        for a in (0, 2, 1, 3):
            x_copy(a // 2, 0, a).wait_recv()
            fk_copy(a).start()
        for a in range(4):
            sides[a, 0], sides[a, 1] = value_sides(0, a)
        for a in range(4):
            arrived(qbuf.at[a], e_recv.at[2, a])
            both = qbuf[a].astype(F32).reshape(256, 128)
            lo = jnp.where(lane256, both, 0.0)
            hi = jnp.where(lane256, 0.0, both)
            qlo[a, 0:256] = lo.astype(BF16)
            qlo[a, 256:512] = pltpu.roll(hi, HD, 1).astype(BF16)
            qhi[a, 0:256] = pltpu.roll(lo, HD, 1).astype(BF16)
            qhi[a, 256:512] = hi.astype(BF16)

    for dx in range(1, 4):
        for r in range(1, 4):
            w1_copy(dx, r).start()

    def update(a, blocks, first):
        scores = []
        for buf, ap, _ in blocks:
            keys = kbuf[buf, ap].reshape(256, 128)
            for q in (qlo, qhi):
                scores.append(
                    lax.dot_general(q[a], keys, (((1,), (1,)), ((), ())), preferred_element_type=F32)
                )
        weights = []
        alphas = []
        for n in range(8):
            rows = slice(n * 64, (n + 1) * 64)
            cols = []
            for b, (_, _, midx) in enumerate(blocks):
                for half in range(2):
                    for jt in range(2):
                        hide = tiles[midx, n % 4, jt][None]
                        tile = scores[2 * b + half][rows, jt * 128:(jt + 1) * 128]
                        cols.append((tile.reshape(8, 8, 128) + hide).reshape(64, 128))
            top = jnp.max(functools.reduce(jnp.maximum, cols), axis=1, keepdims=True)
            if first:
                m_new = jnp.broadcast_to(top, (64, 128))
            else:
                m_old = m_ref[a, rows]
                m_new = jnp.maximum(m_old, top)
                alphas.append(jnp.exp2((m_old - m_new) * SCALE2))
            m_ref[a, rows] = m_new
            weights.append(
                jnp.concatenate([jnp.exp2((tile - m_new) * SCALE2).astype(BF16) for tile in cols], axis=1)
            )
        values = [sides[ap] if first else value_sides(buf, ap) for buf, ap, _ in blocks]
        for half in range(2):
            rows = slice(half * 256, (half + 1) * 256)
            left_side = jnp.concatenate(weights[4 * half:4 * half + 4], axis=0)
            right_side = jnp.concatenate([v[half] for v in values], axis=0)
            new = jnp.dot(left_side, right_side, preferred_element_type=F32)
            if not first:
                new = acc_ref[a, rows] * jnp.concatenate(alphas[4 * half:4 * half + 4], axis=0) + new
            acc_ref[a, rows] = new

    def local(a):
        blocks = []
        for ap in range(4):
            off = ap - a
            midx = jnp.where(off > 0, 4 + 2 * off, 3 - 2 * off)
            midx = jnp.where(off == 0, 0, midx)
            blocks.append((0, ap, jnp.where((off > 2) | (off < -2), 9, midx)))
        update(a, blocks, True)

    def pair(buf_minus, buf_plus, step_minus, step_plus, midx):
        def body(a):
            minus, plus = a - step_minus, a + step_plus
            update(
                a,
                [
                    (buf_minus, jnp.maximum(minus, 0), jnp.where(minus >= 0, midx, 9)),
                    (buf_plus, jnp.minimum(plus, 3), jnp.where(plus <= 3, midx + 1, 9)),
                ],
                False,
            )

        return body

    near = pair(1, 2, (3 - x) // 3, (x + 1) // 4, 1)
    far = pair(3, 3, (3 - x) // 2, (x + 2) // 4, 3)

    def hand_over(a):
        lo, hi = acc_ref[a, 0:256], acc_ref[a, 256:512]
        total = pltpu.roll(jnp.where(lane256, hi, lo), HD, 1)
        packed = (jnp.where(lane256, lo, hi) / total).astype(BF16)
        slot = zh * 3 + k_me
        for hd in range(2):
            opack[2 * a + hd] = packed[hd * 128:(hd + 1) * 128]
            here = (a_me == a) & (zh == hd)
            src, dst = opack.at[2 * a + hd], attended.at[0, slot]

            @pl.when(jnp.logical_not(here))
            def _():
                remote(src, dst, o_send, o_recv.at[slot], (a * 4 + x, hd * 8 + y * 2 + c)).start()

            @pl.when(here)
            def _():
                pltpu.make_async_copy(src, dst, o_recv.at[slot]).start()

    def w3_begin():
        @pl.when(jnp.logical_not(boundary))
        def _():
            w2_copy(0).wait_recv()
            w2_copy(1).wait_recv()

        w3_copy(0).start()
        w3_copy(1).start()

    def local_pass(a, carry):
        local(a)
        for b in range(4):

            @pl.when(a == b)
            def _():
                pass_values(b)
                if b in (0, 2):
                    w2_forward(b // 2)

        return carry

    def near_pass(a, carry):
        near(a)
        return carry

    def far_pass(n, carry):
        a = (a_me + 4 - n) % 4
        far(a)
        hand_over(a)
        return carry

    @pl.when(active)
    def _():
        lax.fori_loop(0, 4, local_pass, 0)
        for a in range(4):
            x_copy(1 - a // 2, 0, a).wait_recv()
        lax.fori_loop(0, 4, near_pass, 0)
        for a in range(4):
            fk_copy(a).wait_recv()
            got_values(a)
        w3_begin()
        lax.fori_loop(0, 4, far_pass, 0)

    @pl.when(jnp.logical_not(active))
    def _():
        w2_forward(0)
        w2_forward(1)
        w3_begin()

    def a_copy(r, slot):
        return remote(
            attended.at[0, slot], attended.at[r, slot], a_send.at[r - 1, slot], a_recv.at[r - 1, slot],
            (seq, zh * 8 + ((y + r) % 4) * 2 + c),
        )

    def gather(step):
        zs = (zh * 4 + a_me + step) % 8
        k = (zs % 4 + 7 - y) % 4
        slot = zs // 4 * 3 + k

        @pl.when(k < 3)
        def _():
            arrived(attended.at[0, slot], o_recv.at[slot])
            for r in (2, 1, 3):
                a_copy(r, slot).start()

    def w3_forward():
        for direction in range(2):
            w3_copy(direction).wait_recv()
            w3f_copy(direction).start()

    for step in (0, 4, 1, 5, 2, 6, 3, 7):
        gather(step)
    w3_forward()

    lane128 = lax.broadcasted_iota(jnp.int32, (128, 128), 1) < HD

    def unpack(r):
        for t in range(3):
            x0 = attended[r, 2 * t].astype(F32)
            x1 = attended[r, 2 * t + 1].astype(F32)
            cols = slice(r * 384 + t * 128, r * 384 + (t + 1) * 128)
            lo = jnp.where(lane128, x0, pltpu.roll(x1, HD, 1)).astype(BF16).reshape(4, 2, 16, 128)
            hi = jnp.where(lane128, pltpu.roll(x0, HD, 1), x1).astype(BF16).reshape(4, 2, 16, 128)
            for cd in range(2):
                lhs[cd, :, 0, :, cols] = lo[:, cd]
                lhs[cd, :, 1, :, cols] = hi[:, cd]

    unpack(0)
    for r in (1, 3):
        for slot in range(6):
            a_copy(r, slot).wait_recv()
        unpack(r)
    for direction in range(2):
        w3f_copy(direction).wait_recv()
    for dx in range(1, 4):
        for r in range(1, 4):
            w1_copy(dx, r).wait()

    owners = (y, (y + 3) % 4, (y + 2) % 4, (y + 1) % 4)

    def project(core, n, sources):
        rows = lhs[core].reshape(128, 1536)
        res = None
        for r in sources:
            rhs = wbuf[owners[r], :, :, n * 256:(n + 1) * 256].reshape(384, 256)
            d = jnp.dot(rows[:, r * 384:(r + 1) * 384], rhs, preferred_element_type=F32)
            res = d if res is None else res + d
        return res

    for n in range(3):
        part[n] = project(1 - c, n, (0, 1, 3))
        mine[n] = project(c, n, (0, 1, 3))
    @pl.when(active)
    def _():
        arrived(sendbuf.at[pl.ds(0, 141)], e_send)
        for t in range(2):
            for a in range(4):
                x_copy(0, t, a).wait_send()
                x_copy(1, t, a).wait_send()
        for a in range(4):
            fk_copy(a).wait_send()
            fv_copy(0, a).wait_send()
            fv_copy(1, a).wait_send()
        arrived(opack.at[pl.ds(0, 7)], o_send)

    @pl.when(boundary)
    def _():
        for n in range(2):
            w2_copy(n).wait_send()
            w2f_copy(n).wait_send()

    for direction in range(2):
        w3_copy(direction).wait_send()
        w3f_copy(direction).wait_send()
    for slot in range(6):
        a_copy(2, slot).wait_recv()
    unpack(2)

    def d_copy(n):
        return remote(part.at[n], dpart.at[n], d_send.at[n], d_recv.at[n], (seq, g + 1 - 2 * c))

    def y_copy(n, r):
        yd = (y + r) % 4
        cols = pl.ds(pl.multiple_of(y * 768 + n * 256, 128), 256)
        return remote(
            fin.at[n, yd], o_ref.at[:, cols], y_send.at[n, r - 1], y_recv.at[n, r - 1],
            (seq, zh * 8 + yd * 2 + c),
        )

    for n in range(3):
        part[n] += project(1 - c, n, (2,))
        d_copy(n).start()
    for n in range(3):
        total = mine[n] + project(c, n, (2,))
        cols = pl.ds(pl.multiple_of(y * 768 + n * 256, 128), 256)
        d_copy(n).wait_recv()
        done = (total + dpart[n] + bias_ref[cols].astype(F32)[None]).astype(BF16)
        fin[n] = done.reshape(4, 32, 256)
        for r in range(1, 4):
            y_copy(n, r).start()
        o_ref[:, cols] = fin[n, y]

    for r in range(1, 4):
        for slot in range(6):
            a_copy(r, slot).wait_send()
    for n in range(3):
        d_copy(n).wait_send()
        for r in range(1, 4):
            y_copy(n, r).wait()


def shards(query_in, key_in, value_in, block_mask, out_weight, out_bias):
    hbm = pl.BlockSpec(memory_space=pltpu.HBM)
    dma = pltpu.SemaphoreType.DMA
    return pl.pallas_call(
        kernel,
        out_shape=jax.ShapeDtypeStruct((32, 3072), BF16),
        in_specs=[hbm] * 6,
        out_specs=pl.BlockSpec(memory_space=pltpu.VMEM),
        scratch_shapes=[
            pltpu.VMEM((3, 32, 3072), BF16),
            pltpu.SMEM((4, 4, 9), jnp.int32),
            pltpu.VMEM((3072,), BF16),
            pltpu.VMEM((144, 16, 128), BF16),
            pltpu.VMEM((4, 4, 16, 16, 128), BF16),
            pltpu.VMEM((4, 4, 16, 16, 128), BF16),
            pltpu.VMEM((4, 16, 16, 128), BF16),
            pltpu.VMEM((4, 512, 128), BF16),
            pltpu.VMEM((4, 512, 128), BF16),
            pltpu.VMEM((10, 4, 2, 8, 128), F32),
            pltpu.VMEM((4, 2, 512, 128), BF16),
            pltpu.VMEM((4, 512, 128), F32),
            pltpu.VMEM((4, 512, 128), F32),
            pltpu.VMEM((8, 128, 128), BF16),
            pltpu.VMEM((4, 6, 128, 128), BF16),
            pltpu.VMEM((2, 4, 2, 16, 1536), BF16),
            pltpu.VMEM((4, 2, 192, 768), BF16),
            pltpu.VMEM((3, 128, 256), F32),
            pltpu.VMEM((3, 128, 256), F32),
            pltpu.VMEM((3, 128, 256), F32),
            pltpu.VMEM((3, 4, 32, 256), BF16),
            dma((5,)), dma, dma((3, 4)), dma((2, 2, 4)), dma((2, 2, 4)), dma((4,)), dma((4,)), dma((2, 4)), dma((2, 4)),
            dma((4, 3)), dma((4, 3)), dma, dma((2,)), dma((2,)), dma((2,)), dma((2,)), dma((2,)), dma((2,)), dma((2,)),
            dma, dma((6,)), dma((3, 6)), dma((3, 6)),
            dma((3,)), dma((3,)), dma((3, 3)), dma((3, 3)),
        ],
        compiler_params=pltpu.CompilerParams(
            collective_id=0, has_side_effects=True, vmem_limit_bytes=63 * 1024 * 1024
        ),
        name="radial",
    )(query_in, key_in, value_in, jnp.transpose(block_mask, (1, 2, 0)), out_weight, out_bias)


def solution(mesh):
    return jax.shard_map(
        shards,
        mesh=mesh,
        in_specs=(
            P(("seq", "head"), None),
            P(("seq", "head"), None),
            P(("seq", "head"), None),
            P(),
            P("head", None),
            P(),
        ),
        out_specs=P(("seq", "head"), None),
        check_vma=False,
    )
```

time: 70.5 us -> 66.4 us (0.942)
  Pallas kernels: 68.8 us -> 64.6 us
    pallas_call x1, Pallas kernels: 68.8 us -> 64.6 us  [shards(): pl.pallas_call(kernel, out_shape=jax.ShapeDtypeStruct((32, 3072), BF16),...]
where the time goes in v4:
time: 66.4 us; the launch traced here: 66.2 us
  Pallas kernels  64.6 us (97%)
  local copies, waits for them, and re-layouts  1.62 us (2%)
    pallas_call x1, Pallas kernels, shards(): pl.pallas_call(kernel, out_shape=jax.ShapeDtypeStruct((32, 3072), BF16),...  64.6 us
    unnamed x1, local copies, waits for them, and re-layouts  1.62 us

profile of v4, /device:TPU:1, one launch (start us, length us, event | category | flops | bytes accessed | tf_op | source)
XLA Modules:
  0.0 66.2 jit_solution(17024399292894392843)
XLA Ops:
  0.0 64.6 %radial.1 = bf16[32,3072]{1,0:T(8,128)(2,1)} custom-call(bf16[32,3072]{1,0:T(8,128)(2,1)} %q_hbm.1, bf16[32,3072]{1,0:T(8,128)(2,1)} %k_hbm.1, bf16[32,3072]{1,0:T(8,128)(2,1)} %v_hbm.1, s32[4,4,9]{2,1,0:T(4,128)} %bitcast.1, bf16[192,3072]{1,0:T(8,128)(2,1)} %w_hbm.1, bf16[3072]{0:T(1024)(128)(2,1)} %bias_hbm.1), custom_call_target="tpu_custom_call" | custom-call | tf_op jit(solution)/shard_map/radial/pallas_call | solution.py:502
  64.6 1.6 %copy.8 = bf16[32,3072]{1,0:T(8,128)(2,1)} copy(bf16[32,3072]{1,0:T(8,128)(2,1)} %radial.1) | data formatting | bytes 393216

commit v5 on v4

--- a/solution.py
+++ b/solution.py
@@ -13,13 +13,15 @@
 BF16 = jnp.bfloat16
 HD = 64
 NEG = -1e30
+STEPS = (0, 4, 1, 5, 2, 6, 3, 7)
+LAG = 8
 SCALE2 = math.log2(math.e) / math.sqrt(HD)
 
 
 def kernel(
     q_hbm, k_hbm, v_hbm, mask_hbm, w_hbm, bias_hbm, o_ref,
     raw, mask, bias_ref, sendbuf, kbuf, vbuf, qbuf, qlo, qhi, tiles, sides, m_ref, acc_ref, opack,
-    attended, lhs, wbuf, part, mine, dpart, fin,
+    attended, lhs, wbuf, part, dpart, fin,
     in_sem, e_send, e_recv, x_send, x_recv, fk_send, fk_recv, fv_send, fv_recv,
     w1_send, w1_recv, w1_loc, w2_send, w2_recv, w2f_send, w3_send, w3_recv, w3f_send, w3f_recv,
     o_send, o_recv, a_send, a_recv, d_send, d_recv, y_send, y_recv,
@@ -72,10 +74,7 @@
 
         lax.fori_loop(0, 24, body, 0, unroll=4)
 
-    for t in range(3):
-        prepare(t)
-    fetch[3].wait()
-    fetch[4].wait()
+    prepare(0)
     pl.semaphore_wait(barrier, 65)
 
     def send_wave(t, target):
@@ -113,8 +112,12 @@
     send_wave(0, kbuf.at[0, a_me, g])
     for r in range(1, 4):
         w1_copy(0, r).start()
+    prepare(1)
     send_wave(1, vbuf.at[0, a_me, g])
+    prepare(2)
     send_wave(2, qbuf.at[a_me, g])
+    fetch[3].wait()
+    fetch[4].wait()
 
     def x_copy(direction, t, a):
         buf = (kbuf, vbuf)[t]
@@ -373,70 +376,112 @@
         w2_forward(1)
         w3_begin()
 
-    def a_copy(r, slot):
-        return remote(
-            attended.at[0, slot], attended.at[r, slot], a_send.at[r - 1, slot], a_recv.at[r - 1, slot],
-            (seq, zh * 8 + ((y + r) % 4) * 2 + c),
-        )
-
-    def gather(step):
+    def a_copy(r, slot, h):
+        rows = pl.ds(64 * h, 64)
+        return remote(
+            attended.at[0, slot, rows], attended.at[r, slot, rows],
+            a_send.at[r - 1, slot, h], a_recv.at[r - 1, slot, h], (seq, zh * 8 + ((y + r) % 4) * 2 + c),
+        )
+
+    def gather(step, h):
         zs = (zh * 4 + a_me + step) % 8
         k = (zs % 4 + 7 - y) % 4
         slot = zs // 4 * 3 + k
 
         @pl.when(k < 3)
         def _():
-            arrived(attended.at[0, slot], o_recv.at[slot])
+            if h == 0:
+                arrived(attended.at[0, slot], o_recv.at[slot])
             for r in (2, 1, 3):
-                a_copy(r, slot).start()
+                a_copy(r, slot, h).start()
 
     def w3_forward():
         for direction in range(2):
             w3_copy(direction).wait_recv()
             w3f_copy(direction).start()
 
-    for step in (0, 4, 1, 5, 2, 6, 3, 7):
-        gather(step)
+    for n, step in enumerate(STEPS):
+        gather(step, 0)
+        if n >= LAG:
+            gather(STEPS[n - LAG], 1)
+    for step in STEPS[8 - LAG:]:
+        gather(step, 1)
     w3_forward()
 
-    lane128 = lax.broadcasted_iota(jnp.int32, (128, 128), 1) < HD
-
-    def unpack(r):
+    lane64 = lax.broadcasted_iota(jnp.int32, (64, 128), 1) < HD
+
+    def unpack(r, h):
         for t in range(3):
-            x0 = attended[r, 2 * t].astype(F32)
-            x1 = attended[r, 2 * t + 1].astype(F32)
+            x0 = attended[r, 2 * t, 64 * h:64 * h + 64].astype(F32)
+            x1 = attended[r, 2 * t + 1, 64 * h:64 * h + 64].astype(F32)
             cols = slice(r * 384 + t * 128, r * 384 + (t + 1) * 128)
-            lo = jnp.where(lane128, x0, pltpu.roll(x1, HD, 1)).astype(BF16).reshape(4, 2, 16, 128)
-            hi = jnp.where(lane128, pltpu.roll(x0, HD, 1), x1).astype(BF16).reshape(4, 2, 16, 128)
+            lo = jnp.where(lane64, x0, pltpu.roll(x1, HD, 1)).astype(BF16).reshape(2, 2, 16, 128)
+            hi = jnp.where(lane64, pltpu.roll(x0, HD, 1), x1).astype(BF16).reshape(2, 2, 16, 128)
             for cd in range(2):
-                lhs[cd, :, 0, :, cols] = lo[:, cd]
-                lhs[cd, :, 1, :, cols] = hi[:, cd]
-
-    unpack(0)
-    for r in (1, 3):
-        for slot in range(6):
-            a_copy(r, slot).wait_recv()
-        unpack(r)
-    for direction in range(2):
-        w3f_copy(direction).wait_recv()
-    for dx in range(1, 4):
-        for r in range(1, 4):
-            w1_copy(dx, r).wait()
+                lhs[h, cd, :, 0, :, cols] = lo[:, cd]
+                lhs[h, cd, :, 1, :, cols] = hi[:, cd]
 
     owners = (y, (y + 3) % 4, (y + 2) % 4, (y + 1) % 4)
 
-    def project(core, n, sources):
-        rows = lhs[core].reshape(128, 1536)
+    def project(h, n):
+        rows = lhs[h].reshape(128, 1536)
         res = None
-        for r in sources:
+        for r in range(4):
             rhs = wbuf[owners[r], :, :, n * 256:(n + 1) * 256].reshape(384, 256)
             d = jnp.dot(rows[:, r * 384:(r + 1) * 384], rhs, preferred_element_type=F32)
             res = d if res is None else res + d
-        return res
-
-    for n in range(3):
-        part[n] = project(1 - c, n, (0, 1, 3))
-        mine[n] = project(c, n, (0, 1, 3))
+        part[h, n] = res.reshape(2, 64, 256)
+
+    def d_copy(h, n):
+        return remote(
+            part.at[h, n, 1 - c], dpart.at[h, n], d_send.at[h, n], d_recv.at[h, n], (seq, g + 1 - 2 * c)
+        )
+
+    def y_cols(n):
+        return pl.ds(pl.multiple_of(y * 768 + n * 256, 128), 256)
+
+    def y_copy(yd, n, r):
+        return remote(
+            fin.at[yd, n], o_ref.at[:, y_cols(n)], y_send.at[yd, n], y_recv.at[r, n],
+            (seq, zh * 8 + yd * 2 + c),
+        )
+
+    def begin_half(h):
+        for r in (1, 3, 2):
+            for slot in range(6):
+                a_copy(r, slot, h).wait_recv()
+            unpack(r, h)
+        if h == 0:
+            for direction in range(2):
+                w3f_copy(direction).wait_recv()
+            for dx in range(1, 4):
+                for r in range(1, 4):
+                    w1_copy(dx, r).wait()
+        for n in range(3):
+            project(h, n)
+            d_copy(h, n).start()
+
+    def end_half(h):
+        for n in range(3):
+            d_copy(h, n).wait_recv()
+            bias = bias_ref[y_cols(n)].astype(F32)[None]
+            done = (part[h, n, c] + dpart[h, n] + bias).astype(BF16).reshape(2, 32, 256)
+            for b in range(2):
+                yd = 2 * h + b
+                fin[yd, n] = done[b]
+
+                @pl.when(y != yd)
+                def _():
+                    y_copy(yd, n, (yd + 4 - y) % 4).start()
+
+                @pl.when(y == yd)
+                def _():
+                    o_ref[:, y_cols(n)] = done[b]
+
+    unpack(0, 0)
+    unpack(0, 1)
+    begin_half(0)
+
     @pl.when(active)
     def _():
         arrived(sendbuf.at[pl.ds(0, 141)], e_send)
@@ -459,41 +504,26 @@
     for direction in range(2):
         w3_copy(direction).wait_send()
         w3f_copy(direction).wait_send()
-    for slot in range(6):
-        a_copy(2, slot).wait_recv()
-    unpack(2)
-
-    def d_copy(n):
-        return remote(part.at[n], dpart.at[n], d_send.at[n], d_recv.at[n], (seq, g + 1 - 2 * c))
-
-    def y_copy(n, r):
-        yd = (y + r) % 4
-        cols = pl.ds(pl.multiple_of(y * 768 + n * 256, 128), 256)
-        return remote(
-            fin.at[n, yd], o_ref.at[:, cols], y_send.at[n, r - 1], y_recv.at[n, r - 1],
-            (seq, zh * 8 + yd * 2 + c),
-        )
-
-    for n in range(3):
-        part[n] += project(1 - c, n, (2,))
-        d_copy(n).start()
-    for n in range(3):
-        total = mine[n] + project(c, n, (2,))
-        cols = pl.ds(pl.multiple_of(y * 768 + n * 256, 128), 256)
-        d_copy(n).wait_recv()
-        done = (total + dpart[n] + bias_ref[cols].astype(F32)[None]).astype(BF16)
-        fin[n] = done.reshape(4, 32, 256)
-        for r in range(1, 4):
-            y_copy(n, r).start()
-        o_ref[:, cols] = fin[n, y]
-
+
+    end_half(0)
+    begin_half(1)
     for r in range(1, 4):
         for slot in range(6):
-            a_copy(r, slot).wait_send()
+            for h in range(2):
+                a_copy(r, slot, h).wait_send()
+    end_half(1)
+
     for n in range(3):
-        d_copy(n).wait_send()
+        for h in range(2):
+            d_copy(h, n).wait_send()
+        for yd in range(4):
+
+            @pl.when(y != yd)
+            def _():
+                y_copy(yd, n, 0).wait_send()
+
         for r in range(1, 4):
-            y_copy(n, r).wait()
+            y_copy(0, n, r).wait_recv()
 
 
 def shards(query_in, key_in, value_in, block_mask, out_weight, out_bias):
@@ -520,16 +550,15 @@
             pltpu.VMEM((4, 512, 128), F32),
             pltpu.VMEM((8, 128, 128), BF16),
             pltpu.VMEM((4, 6, 128, 128), BF16),
-            pltpu.VMEM((2, 4, 2, 16, 1536), BF16),
+            pltpu.VMEM((2, 2, 2, 2, 16, 1536), BF16),
             pltpu.VMEM((4, 2, 192, 768), BF16),
-            pltpu.VMEM((3, 128, 256), F32),
-            pltpu.VMEM((3, 128, 256), F32),
-            pltpu.VMEM((3, 128, 256), F32),
-            pltpu.VMEM((3, 4, 32, 256), BF16),
+            pltpu.VMEM((2, 3, 2, 64, 256), F32),
+            pltpu.VMEM((2, 3, 64, 256), F32),
+            pltpu.VMEM((4, 3, 32, 256), BF16),
             dma((5,)), dma, dma((3, 4)), dma((2, 2, 4)), dma((2, 2, 4)), dma((4,)), dma((4,)), dma((2, 4)), dma((2, 4)),
             dma((4, 3)), dma((4, 3)), dma, dma((2,)), dma((2,)), dma((2,)), dma((2,)), dma((2,)), dma((2,)), dma((2,)),
-            dma, dma((6,)), dma((3, 6)), dma((3, 6)),
-            dma((3,)), dma((3,)), dma((3, 3)), dma((3, 3)),
+            dma, dma((6,)), dma((3, 6, 2)), dma((3, 6, 2)),
+            dma((2, 3)), dma((2, 3)), dma((4, 3)), dma((4, 3)),
         ],
         compiler_params=pltpu.CompilerParams(
             collective_id=0, has_side_effects=True, vmem_limit_bytes=63 * 1024 * 1024

time: 66.4 us -> 65.6 us (0.988)
  Pallas kernels: 64.6 us -> 63.9 us
    pallas_call x1, Pallas kernels: 64.6 us -> 63.9 us  [shards(): pl.pallas_call(kernel, out_shape=jax.ShapeDtypeStruct((32, 3072), BF16),...]
where the time goes in v5:
time: 65.6 us; the launch traced here: 65.5 us
  Pallas kernels  63.9 us (97%)
  local copies, waits for them, and re-layouts  1.62 us (2%)
    pallas_call x1, Pallas kernels, shards(): pl.pallas_call(kernel, out_shape=jax.ShapeDtypeStruct((32, 3072), BF16),...  63.9 us
    unnamed x1, local copies, waits for them, and re-layouts  1.62 us

profile of v5, /device:TPU:1, one launch (start us, length us, event | category | flops | bytes accessed | tf_op | source)
XLA Modules:
  0.0 65.5 jit_solution(14980693131005270562)
XLA Ops:
  0.0 63.9 %radial.1 = bf16[32,3072]{1,0:T(8,128)(2,1)} custom-call(bf16[32,3072]{1,0:T(8,128)(2,1)} %q_hbm.1, bf16[32,3072]{1,0:T(8,128)(2,1)} %k_hbm.1, bf16[32,3072]{1,0:T(8,128)(2,1)} %v_hbm.1, s32[4,4,9]{2,1,0:T(4,128)} %bitcast.1, bf16[192,3072]{1,0:T(8,128)(2,1)} %w_hbm.1, bf16[3072]{0:T(1024)(128)(2,1)} %bias_hbm.1), custom_call_target="tpu_custom_call" | custom-call | tf_op jit(solution)/shard_map/radial/pallas_call | solution.py:532
  63.9 1.6 %copy.8 = bf16[32,3072]{1,0:T(8,128)(2,1)} copy(bf16[32,3072]{1,0:T(8,128)(2,1)} %radial.1) | data formatting | bytes 393216

commit v6 on v5

--- a/solution.py
+++ b/solution.py
@@ -284,13 +284,23 @@
             acc_ref[a, rows] = new
 
     def local(a):
-        blocks = []
-        for ap in range(4):
-            off = ap - a
-            midx = jnp.where(off > 0, 4 + 2 * off, 3 - 2 * off)
-            midx = jnp.where(off == 0, 0, midx)
-            blocks.append((0, ap, jnp.where((off > 2) | (off < -2), 9, midx)))
-        update(a, blocks, True)
+        def some(first, count):
+            blocks = []
+            for step in range(count):
+                off = first + step - a
+                midx = jnp.where(off > 0, 4 + 2 * off, 3 - 2 * off)
+                blocks.append((0, first + step, jnp.where(off == 0, 0, midx)))
+            update(a, blocks, True)
+
+        outer = (a == 0) | (a == 3)
+
+        @pl.when(outer)
+        def _():
+            some(a // 3, 3)
+
+        @pl.when(jnp.logical_not(outer))
+        def _():
+            some(0, 4)
 
     def pair(buf_minus, buf_plus, step_minus, step_plus, midx):
         def body(a):
@@ -338,13 +348,15 @@
 
     def local_pass(a, carry):
         local(a)
-        for b in range(4):
+        for b in range(1, 4):
 
             @pl.when(a == b)
             def _():
+                if b == 1:
+                    pass_values(0)
                 pass_values(b)
-                if b in (0, 2):
-                    w2_forward(b // 2)
+                if b < 3:
+                    w2_forward(b - 1)
 
         return carry
 

time: 65.6 us -> 65.4 us (level)
  no operation moved by 1% of the time
where the time goes in v6:
time: 65.4 us; the launch traced here: 65.2 us
  Pallas kernels  63.5 us (97%)
  local copies, waits for them, and re-layouts  1.62 us (2%)
    pallas_call x1, Pallas kernels, shards(): pl.pallas_call(kernel, out_shape=jax.ShapeDtypeStruct((32, 3072), BF16),...  63.5 us
    unnamed x1, local copies, waits for them, and re-layouts  1.62 us

profile of v6, /device:TPU:1, one launch (start us, length us, event | category | flops | bytes accessed | tf_op | source)
XLA Modules:
  0.0 65.2 jit_solution(12770411052560775276)
XLA Ops:
  0.0 63.5 %radial.1 = bf16[32,3072]{1,0:T(8,128)(2,1)} custom-call(bf16[32,3072]{1,0:T(8,128)(2,1)} %q_hbm.1, bf16[32,3072]{1,0:T(8,128)(2,1)} %k_hbm.1, bf16[32,3072]{1,0:T(8,128)(2,1)} %v_hbm.1, s32[4,4,9]{2,1,0:T(4,128)} %bitcast.1, bf16[192,3072]{1,0:T(8,128)(2,1)} %w_hbm.1, bf16[3072]{0:T(1024)(128)(2,1)} %bias_hbm.1), custom_call_target="tpu_custom_call" | custom-call | tf_op jit(solution)/shard_map/radial/pallas_call | solution.py:544
  63.6 1.6 %copy.8 = bf16[32,3072]{1,0:T(8,128)(2,1)} copy(bf16[32,3072]{1,0:T(8,128)(2,1)} %radial.1) | data formatting | bytes 393216
